TPU v7x, 128 devices: a whole 4x4x4 slice. The times are simulated.
128 devices in a mesh: frame: 4 (over z), patch: 32 (over x, y, core).
Axes of the slice: x: 4, y: 4, z: 4, core: 2. Of those that a mesh axis runs over, the one named last changes fastest.
Arguments:
- video: bfloat16 [8, 2048, 1152], P('frame', 'patch'), may hold values from -6 to 6
- cotangent: bfloat16 [8, 2048, 1152], P('frame', 'patch'), may hold values from -6 to 6
- frame_mask: int32 [8], replicated, may hold values 0 or 1
- spatial_project: bfloat16 [1152, 3456], replicated, may hold values from -0.1875 to 0.1875
- spatial_output: bfloat16 [1152, 1152], replicated, may hold values from -0.1875 to 0.1875
- temporal_project: bfloat16 [1152, 3456], replicated, may hold values from -0.1875 to 0.1875
- temporal_output: bfloat16 [1152, 1152], replicated, may hold values from -0.1875 to 0.1875
- spatial_inward: float32 [36, 32, 32], replicated, may hold values from -0.25 to 1.25, as said below
- spatial_outward: float32 [36, 32, 32], replicated, may hold values from -0.25 to 1.25, as said below
- temporal_inward: float32 [36, 32, 32], replicated, may hold values from -0.25 to 1.25, as said below
- temporal_outward: float32 [36, 32, 32], replicated, may hold values from -0.25 to 1.25, as said below
Outputs:
- video_gradient: bfloat16 [8, 2048, 1152], P('frame', 'patch')
- gradient_spatial_inward: float32 [36, 32, 32], replicated
- gradient_spatial_outward: float32 [36, 32, 32], replicated
- gradient_temporal_inward: float32 [36, 32, 32], replicated
- gradient_temporal_outward: float32 [36, 32, 32], replicated
Inputs may be any that keep to these rules, and one draw needn't show every extreme that they name: `spatial_inward`: identity blocks plus independent entries. `spatial_outward`: identity blocks plus independent entries. `temporal_inward`: identity blocks plus independent entries. `temporal_outward`: identity blocks plus independent entries.
All inputs are finite; a program needn't handle non-finite values.
Results may differ from a plain program's by a relative error of at most 0.028.
Values may be sent and summed in bfloat16 or wider, within the bound.
A program may use at most 192 MiB of HBM per device.

v0:
```python
import functools
import math

import jax
import jax.numpy as jnp
from jax import lax
from jax.experimental import pallas as pl
from jax.experimental.pallas import tpu as pltpu
from jax.sharding import PartitionSpec as P

D = 1152
HEADS = 16
HEAD_DIM = 72
BLOCK = 32
GROUPS = D // 128
FRAMES = 8
PATCHES = 2048
ZWAYS = 4
PWAYS = 32
DEVICES = ZWAYS * PWAYS
TOKENS = 128
ROWS = D // 4

EPSILON = 1e-06
NEGATIVE = -1e30
SCALE = 1.0 / math.sqrt(HEAD_DIM)
LOG2E = math.log2(math.e)
LN2 = math.log(2.0)

F32 = jnp.float32
BF16 = jnp.bfloat16
MESH = pl.DeviceIdType.MESH


def dot(a, b):
    return lax.dot_general(a, b, (((1,), (0,)), ((), ())), preferred_element_type=F32)


def dot_nt(a, b):
    return lax.dot_general(a, b, (((1,), (1,)), ((), ())), preferred_element_type=F32)


def dot_tn(a, b):
    return lax.dot_general(a, b, (((0,), (0,)), ((), ())), preferred_element_type=F32)


def lanes(shape):
    return lax.broadcasted_iota(jnp.int32, shape, len(shape) - 1)


def rows(shape):
    return lax.broadcasted_iota(jnp.int32, shape, 0)


def roll(x, amount):
    amount = amount % 128
    return x if amount == 0 else pltpu.roll(x, amount, 1)


def normalize(x):
    centered = x - jnp.mean(x, axis=-1, keepdims=True)
    inverse = lax.rsqrt(jnp.mean(centered * centered, axis=-1, keepdims=True) + EPSILON)
    return centered * inverse, inverse


def normalize_backward(adjoint, normed, inverse):
    grad_mean = jnp.mean(adjoint, axis=-1, keepdims=True)
    grad_cross = jnp.mean(adjoint * normed, axis=-1, keepdims=True)
    return inverse * (adjoint - grad_mean - normed * grad_cross)


def group(x, g):
    return x[:, g * 128 : (g + 1) * 128]


def rotate(x, blocks):
    return jnp.concatenate(
        [dot(group(x, g), blocks[g * 128 : (g + 1) * 128, :]) for g in range(GROUPS)], axis=1
    )


def rotate_transposed(x, blocks):
    return jnp.concatenate(
        [dot_nt(group(x, g), blocks[g * 128 : (g + 1) * 128, :]) for g in range(GROUPS)], axis=1
    )


def block_mask(shape):
    return (rows(shape) // BLOCK) % 4 == lanes(shape) // BLOCK


def rotation_gradient(left, right):
    mask = block_mask((128, 128))
    packed = []
    for g in range(GROUPS):
        full = jnp.where(mask, dot_tn(group(left, g), group(right, g)), 0.0)
        packed.append(full[0:32] + full[32:64] + full[64:96] + full[96:128])
    return packed


def kernel(
    mask_ref, video, cotangent, wsp_h, wso_h, wtp_h, wto_h, rsi_h, rso_h, rti_h, rto_h,
    vg_ref, red_ref,
    wsp, wso, wtp, wto, r4, bd,
    vid, cot, vid_mid, ct_mid,
    normed1, inverse1, proj,
    qkv_snd, qkv_rcv, kx, qx,
    att_snd, att_rcv, att1, top, aot, daz,
    hidp, normed2, proj2, dproj, att2, dproj_b,
    ah_snd, ah_rcv, do_snd, do_rcv, vx, dox, dosh, qsh, kt, dqt, dkv,
    dq_snd, dq_rcv,
    r1_snd, r1_rcv, r1_z, r1_chunk, r1_out,
    r2_snd, r2_rcv, r2_z, r2_chunk, r2_out,
    wsem, vsem, send_sems, recv_sems,
):
    z = lax.axis_index("frame")
    j = lax.axis_index("patch")
    me = z * PWAYS + j

    loads = [
        pltpu.make_async_copy(video, vid, wsem.at[0]),
        pltpu.make_async_copy(rsi_h, r4.at[0], wsem.at[1]),
        pltpu.make_async_copy(wsp_h, wsp, wsem.at[2]),
        pltpu.make_async_copy(cotangent, cot, wsem.at[3]),
        pltpu.make_async_copy(rso_h, r4.at[1], wsem.at[4]),
        pltpu.make_async_copy(rti_h, r4.at[2], wsem.at[5]),
        pltpu.make_async_copy(rto_h, r4.at[3], wsem.at[6]),
        pltpu.make_async_copy(wto_h, wto, wsem.at[7]),
        pltpu.make_async_copy(wso_h, wso, wsem.at[8]),
        pltpu.make_async_copy(wtp_h, wtp, wsem.at[9]),
    ]
    for load in loads:
        load.start()

    barrier = pltpu.get_barrier_semaphore()

    def greet(i, carry):
        there = lax.rem(me + i, DEVICES)
        pl.semaphore_signal(
            barrier, inc=1, device_id=(there // PWAYS, lax.rem(there, PWAYS)), device_id_type=MESH
        )
        return carry

    lax.fori_loop(1, DEVICES, greet, 0)

    def push(src, dst, phase, zz, jj):
        self_ = jnp.logical_and(zz == z, jj == j)

        @pl.when(self_)
        def _():
            pltpu.make_async_copy(src, dst, recv_sems.at[phase]).start()

        @pl.when(jnp.logical_not(self_))
        def _():
            pltpu.make_async_remote_copy(
                src_ref=src, dst_ref=dst, send_sem=send_sems.at[phase],
                recv_sem=recv_sems.at[phase], device_id=(zz, jj), device_id_type=MESH,
            ).start()

    def wait_all(sem, buffer):
        pltpu.make_async_copy(buffer, buffer, sem).wait()

    def make_blocks(index):
        tile = jnp.where(
            lax.rem(lanes((BLOCK, 128)), BLOCK) == rows((BLOCK, 128)), 1.0, 0.0
        ).astype(BF16)
        wide = dot(r4[index].astype(BF16), tile)
        bd[index] = jnp.where(block_mask((D, 128)), wide, 0.0).astype(BF16)

    loads[0].wait()
    normed, inverse = normalize(vid[...].reshape(TOKENS, D).astype(F32))
    normed1[...] = normed
    inverse1[...] = inverse
    loads[1].wait()
    make_blocks(0)
    rotated = rotate(normed1[...].astype(BF16), bd.at[0]).astype(BF16)
    dproj_b[:, 0:D] = rotated

    pl.semaphore_wait(barrier, DEVICES - 1)

    def spread(i, carry):
        zz = lax.rem(z + i, ZWAYS)
        for f in range(2):
            push(vid.at[f, pl.ds(pl.multiple_of(zz * 16, 16), 16)], vid_mid.at[2 * z + f], 0, zz, j)
        return carry

    lax.fori_loop(0, ZWAYS, spread, 0)
    loads[3].wait()

    def spread_ct(i, carry):
        zz = lax.rem(z + i, ZWAYS)
        for f in range(2):
            push(cot.at[f, pl.ds(pl.multiple_of(zz * 16, 16), 16)], ct_mid.at[2 * z + f], 1, zz, j)
        return carry

    lax.fori_loop(0, ZWAYS, spread_ct, 0)

    loads[2].wait()

    def project1(c, carry):
        at = pl.ds(pl.multiple_of(c * D, 128), D)
        proj[:, at] = dot(dproj_b[:, 0:D], wsp[:, at])
        return carry

    lax.fori_loop(0, 3, project1, 0)

    lane = lanes((TOKENS, 128))
    qscale = jnp.where(lane < HEAD_DIM, SCALE * LOG2E, 1.0)
    for h in range(HEADS):
        t, off = (HEAD_DIM * h) // 128, (HEAD_DIM * h) % 128

        def pick(section, to):
            first = proj[:, section * D + t * 128 : section * D + (t + 1) * 128]
            if off + HEAD_DIM > 128:
                second = proj[:, section * D + (t + 1) * 128 : section * D + (t + 2) * 128]
                first = jnp.where(lane >= off, first, second)
            return roll(first, to - off)

        q, k, v = pick(0, 0), pick(1, 72), pick(2, 16)
        low = (jnp.where(lane < 72, q, k) * qscale).astype(BF16)
        high = jnp.where(
            lane < 16, k, jnp.where(lane < 88, v, jnp.where(lane < 92, 1.0, 0.0))
        ).astype(BF16)
        for f in range(2):
            qkv_snd[f * HEADS + h, :, 0:128] = low[64 * f : 64 * (f + 1)]
            qkv_snd[f * HEADS + h, :, 128:256] = high[64 * f : 64 * (f + 1)]

    def send_qkv(i, carry):
        jj = lax.rem(j + i, PWAYS)
        push(qkv_snd.at[jj], qkv_rcv.at[pl.ds(pl.multiple_of(j * 64, 64), 64)], 2, z, jj)
        return carry

    lax.fori_loop(0, PWAYS, send_qkv, 0)

    for i in (4, 5, 6):
        loads[i].wait()
    make_blocks(1)
    make_blocks(2)
    make_blocks(3)
    wait_all(recv_sems.at[1], ct_mid)
    frame_row = rows((TOKENS, 1)) // 16
    valid = jnp.zeros((TOKENS, 1), F32)
    for f in range(FRAMES):
        valid = jnp.where(frame_row == f, mask_ref[f].astype(F32), valid)
    top[...] = ct_mid[...].reshape(TOKENS, D).astype(F32) * valid
    loads[7].wait()
    aot[...] = dot_nt(top[...].astype(BF16), wto[...]).astype(BF16)
    daz[:, 0:D] = rotate_transposed(aot[...], bd.at[3]).astype(BF16)
    daz[:, D:] = jnp.zeros((TOKENS, 128), BF16)

    wait_all(recv_sems.at[2], qkv_rcv)

    def prepare(i, carry):
        at = pl.ds(pl.multiple_of(i * 256, 256), 256)
        block = qkv_rcv[at, :].astype(F32)
        lane2 = lanes((256, 128))
        t0, t1 = block[:, 0:128], block[:, 128:256]
        k = roll(jnp.where(lane2 >= 72, t0, t1), -72)
        ones = jnp.where(jnp.logical_and(lane2 >= 72, lane2 < 76), 1.0, 0.0)
        kk = jnp.where(lane2 < 72, k, ones)
        kx[at, :] = kk.astype(BF16)
        v = roll(t1, -16)
        vx[at, :] = jnp.where(lane2 < 72, v, ones).astype(BF16)
        kt[:, at] = kk.T.astype(BF16)
        q = jnp.where(lane2 < 72, t0, 0.0)
        qx[at, :] = q.astype(BF16)
        q = roll(q, 72)
        qsh[at, 0:128] = jnp.where(lane2 >= 72, q, 0.0).astype(BF16)
        qsh[at, 128:256] = jnp.where(lane2 < 16, q, 0.0).astype(BF16)
        return carry

    lax.fori_loop(0, 8, prepare, 0)

    def attend(i, carry):
        at = pl.ds(pl.multiple_of(i * 256, 256), 256)
        scores = dot_nt(qx[at, :], kx[...])
        top_score = jnp.max(scores, axis=-1, keepdims=True)
        p = jnp.exp2(scores - top_score).astype(BF16)
        out = dot(p, vx[...])
        total = out[:, 72:73]
        lane2 = lanes((256, 128))
        att_snd[at, :] = jnp.where(lane2 < 72, out / total, 0.0).astype(BF16)
        neg = -(top_score + jnp.log(total) * LOG2E)
        hi = neg.astype(BF16).astype(F32)
        mid = (neg - hi).astype(BF16).astype(F32)
        lo = neg - hi - mid
        old = qx[at, :].astype(F32)
        new = jnp.where(lane2 == 72, hi, jnp.where(lane2 == 73, mid, jnp.where(lane2 == 74, lo, old)))
        qx[at, :] = new.astype(BF16)

        def send(s, c):
            there = i * 16 + s
            push(
                att_snd.at[pl.ds(pl.multiple_of(there * 16, 16), 16)],
                att_rcv.at[2 * z + j // HEADS, lax.rem(j, HEADS)],
                3, lax.rem(there, ZWAYS), there // ZWAYS,
            )
            return c

        lax.fori_loop(0, 16, send, 0)
        return carry

    lax.fori_loop(0, 8, attend, 0)

    wait_all(recv_sems.at[0], vid_mid)
    wait_all(recv_sems.at[3], att_rcv)
    tiles = [None] * (GROUPS + 1)
    for h in range(HEADS):
        t, off = (HEAD_DIM * h) // 128, (HEAD_DIM * h) % 128
        r = roll(att_rcv[:, h].reshape(TOKENS, 128).astype(F32), off)
        if off + HEAD_DIM > 128:
            pieces = [(t, jnp.where(lane >= off, r, 0.0)), (t + 1, jnp.where(lane < off, r, 0.0))]
        else:
            pieces = [(t, r)]
        for at, piece in pieces:
            tiles[at] = piece if tiles[at] is None else tiles[at] + piece
    for t in range(GROUPS):
        att1[:, t * 128 : (t + 1) * 128] = tiles[t].astype(BF16)

    loads[8].wait()
    outrot = rotate(att1[...], bd.at[1]).astype(BF16)
    hidden = vid_mid[...].reshape(TOKENS, D).astype(F32) + dot(outrot, wso[...])
    hidden = hidden.astype(BF16).astype(F32)
    normed, inverse2 = normalize(hidden)
    normed2[...] = normed
    dproj_b[:, 0:D] = rotate(normed.astype(BF16), bd.at[2]).astype(BF16)
    loads[9].wait()

    def project2(c, carry):
        at = pl.ds(pl.multiple_of(c * D, 128), D)
        proj2[:, at] = dot(dproj_b[:, 0:D], wtp[:, at]).astype(BF16)
        return carry

    lax.fori_loop(0, 3, project2, 0)
    proj2[:, 3 * D :] = jnp.zeros((TOKENS, 128), BF16)

    square = (TOKENS, TOKENS)
    same_patch = lax.rem(rows(square), 16) == lax.rem(lanes(square), 16)
    same_frame = rows(square) // 16 == lanes(square) // 16
    key_valid = jnp.zeros(square, F32)
    for f in range(FRAMES):
        key_valid = jnp.where(lanes(square) // 16 == f, mask_ref[f].astype(F32), key_valid)
    allowed = jnp.logical_and(same_patch, jnp.logical_or(key_valid == 1.0, same_frame))
    bias = jnp.where(allowed, 0.0, NEGATIVE)

    dproj[...] = jnp.zeros_like(dproj)
    att2[...] = jnp.zeros_like(att2)
    lane4 = lanes((1, 256))
    for h in range(HEADS):
        t, off = (HEAD_DIM * h) // 128, (HEAD_DIM * h) % 128
        win = slice(t * 128, t * 128 + 256)
        kwin = slice(D + t * 128, D + t * 128 + 256)
        vwin = slice(2 * D + t * 128, 2 * D + t * 128 + 256)
        own = jnp.logical_and(lane4 >= off, lane4 < off + HEAD_DIM)
        own_f = jnp.where(own, 1.0, 0.0)
        own_b = own_f.astype(BF16)
        q = proj2[:, win] * own_b
        k = proj2[:, kwin]
        v = proj2[:, vwin]
        g = daz[:, win] * own_b
        scores = dot_nt(q, k) * SCALE + bias
        e = jnp.exp(scores - jnp.max(scores, axis=-1, keepdims=True))
        p = e / jnp.sum(e, axis=-1, keepdims=True)
        pb = p.astype(BF16)
        att2[:, win] += dot(pb, v) * own_f
        dproj[:, vwin] += dot_tn(pb, g)
        dp = dot_nt(g, v)
        ds = (p * (dp - jnp.sum(p * dp, axis=-1, keepdims=True))).astype(BF16)
        dproj[:, win] += dot(ds, k) * (own_f * SCALE)
        dproj[:, kwin] += dot_tn(ds, q) * SCALE

    dproj_b[...] = dproj[:, 0 : 3 * D].astype(BF16)
    hidp[...] = jnp.zeros_like(hidp)

    def back2(c, carry):
        at = pl.ds(pl.multiple_of(c * D, 128), D)
        hidp[...] += dot_nt(dproj_b[:, at], wtp[:, at])
        return carry

    lax.fori_loop(0, 3, back2, 0)
    adj_rot2 = hidp[...].astype(BF16)
    adj_normed = rotate_transposed(adj_rot2, bd.at[2])
    adj_hidden = top[...] + normalize_backward(adj_normed, normed2[...], inverse2)
    adj_hidden_b = adj_hidden.astype(BF16)
    ah_snd[...] = adj_hidden_b.reshape(FRAMES, 16, D)
    aho = dot_nt(adj_hidden_b, wso[...]).astype(BF16)
    adj_att1 = rotate_transposed(aho, bd.at[1])
    for h in range(HEADS):
        t, off = (HEAD_DIM * h) // 128, (HEAD_DIM * h) % 128
        first = group(adj_att1, t)
        if off + HEAD_DIM > 128:
            first = jnp.where(lane >= off, first, group(adj_att1, t + 1))
        piece = jnp.where(lane < 72, roll(first, -off), 0.0).astype(BF16)
        do_snd[:, h] = piece.reshape(FRAMES, 16, 128)

    def send_do(i, carry):
        there = lax.rem(me + i, DEVICES)
        zz, jj = there // PWAYS, lax.rem(there, PWAYS)
        push(
            do_snd.at[2 * zz + jj // HEADS, lax.rem(jj, HEADS)],
            do_rcv.at[pl.ds(pl.multiple_of((4 * j + z) * 16, 16), 16)],
            4, zz, jj,
        )
        return carry

    lax.fori_loop(0, DEVICES, send_do, 0)

    def send_ah(i, carry):
        zz = lax.rem(z + i, ZWAYS)
        for f in range(2):
            push(
                ah_snd.at[2 * zz + f],
                ah_rcv.at[f, pl.ds(pl.multiple_of(z * 16, 16), 16)],
                5, zz, j,
            )
        return carry

    lax.fori_loop(0, ZWAYS, send_ah, 0)

    for n, packed in enumerate((
        rotation_gradient(att1[...], aho),
        rotation_gradient(normed2[...].astype(BF16), adj_rot2),
        rotation_gradient(att2[:, 0:D].astype(BF16), aot[...]),
    )):
        for g in range(GROUPS):
            r1_snd[n * GROUPS + g] = packed[g].astype(BF16)

    def reduce_first(snd, rcv, owners, phase):
        def send(i, carry):
            jj = lax.rem(j + i, PWAYS)

            @pl.when(jj < owners)
            def _():
                push(snd.at[jj], rcv.at[j], phase, z, jj)

            return carry

        lax.fori_loop(0, PWAYS, send, 0)

    def reduce_second(snd, rcv, zbuf, owners, phase):
        @pl.when(j < owners)
        def _():
            wait_all(recv_sems.at[phase], rcv)
            zbuf[z] = jnp.sum(rcv[...].astype(F32), axis=0)

            def send(i, carry):
                zz = lax.rem(z + i, ZWAYS)
                pltpu.make_async_remote_copy(
                    src_ref=zbuf.at[z], dst_ref=zbuf.at[z], send_sem=send_sems.at[phase + 1],
                    recv_sem=recv_sems.at[phase + 1], device_id=(zz, j), device_id_type=MESH,
                ).start()
                return carry

            lax.fori_loop(1, ZWAYS, send, 0)

    def reduce_third(zbuf, chunk, out, owners, phase):
        @pl.when(j < owners)
        def _():
            wait_all(recv_sems.at[phase + 1], zbuf.at[pl.ds(0, ZWAYS - 1)])
            chunk[...] = (((zbuf[0] + zbuf[1]) + (zbuf[2] + zbuf[3])) / 128.0).astype(BF16)

            def send(i, carry):
                push(chunk, out.at[j], phase + 2, z, lax.rem(j + i, PWAYS))
                return carry

            lax.fori_loop(0, PWAYS, send, 0)

    def reduce_sent(snd, zbuf, out, owners, phase):
        @pl.when(j < owners)
        def _():
            wait_all(send_sems.at[phase], snd.at[pl.ds(0, owners - 1)])
            wait_all(send_sems.at[phase + 1], zbuf.at[pl.ds(0, ZWAYS - 1)])

            def one(i, carry):
                wait_all(send_sems.at[phase + 2], out.at[0])
                return carry

            lax.fori_loop(0, PWAYS - 1, one, 0)

        @pl.when(j >= owners)
        def _():
            wait_all(send_sems.at[phase], snd)

    reduce_first(r1_snd, r1_rcv, 27, 7)

    wait_all(recv_sems.at[4], do_rcv)

    def prepare_back(i, carry):
        at = pl.ds(pl.multiple_of(i * 256, 256), 256)
        lane2 = lanes((256, 128))
        g = do_rcv[at, :].astype(F32)
        delta = -jnp.sum(g * att_snd[at, :].astype(F32), axis=-1, keepdims=True)
        hi = delta.astype(BF16).astype(F32)
        lo = delta - hi
        dox[at, :] = jnp.where(lane2 == 72, hi, jnp.where(lane2 == 73, lo, g)).astype(BF16)
        dosh[at, 0:128] = jnp.zeros((256, 128), BF16)
        dosh[at, 128:256] = roll(g, 16).astype(BF16)
        return carry

    lax.fori_loop(0, 8, prepare_back, 0)
    dqt[...] = jnp.zeros_like(dqt)

    def attend_back(i, carry):
        at = pl.ds(pl.multiple_of(i * 256, 256), 256)
        p = jnp.exp2(dot_nt(kx[at, :], qx[...]))
        pb = p.astype(BF16)
        ds = (p * dot_nt(vx[at, :], dox[...])).astype(BF16)
        dkv[at, :] = dot(pb, dosh[...]) + dot(ds, qsh[...])
        dqt[...] += dot(kt[:, at], ds)
        return carry

    lax.fori_loop(0, 8, attend_back, 0)
    reduce_second(r1_snd, r1_rcv, r1_z, 27, 7)

    def finish_back(i, carry):
        at = pl.ds(pl.multiple_of(i * 256, 256), 256)
        lane2 = lanes((256, 128))
        dq = dqt[:, at].T * SCALE
        low = jnp.where(lane2 < 72, dq, dkv[at, 0:128] * LN2)
        high = jnp.where(lane2 < 16, dkv[at, 128:256] * LN2, dkv[at, 128:256])
        dq_snd[at, 0:128] = low.astype(BF16)
        dq_snd[at, 128:256] = high.astype(BF16)

        def send(s, c):
            jj = i * 4 + s
            push(
                dq_snd.at[pl.ds(pl.multiple_of(jj * 64, 64), 64)], dq_rcv.at[j], 6, z, jj
            )
            return c

        lax.fori_loop(0, 4, send, 0)
        return carry

    lax.fori_loop(0, 8, finish_back, 0)
    reduce_third(r1_z, r1_chunk, r1_out, 27, 7)

    wait_all(recv_sems.at[6], dq_rcv)
    tiles = [[None] * (GROUPS + 1) for _ in range(3)]
    for h in range(HEADS):
        t, off = (HEAD_DIM * h) // 128, (HEAD_DIM * h) % 128
        low = jnp.concatenate(
            [dq_rcv[h, :, 0:128], dq_rcv[HEADS + h, :, 0:128]], axis=0
        ).astype(F32)
        high = jnp.concatenate(
            [dq_rcv[h, :, 128:256], dq_rcv[HEADS + h, :, 128:256]], axis=0
        ).astype(F32)
        q = roll(jnp.where(lane < 72, low, 0.0), off)
        k = roll(jnp.where(lane >= 72, low, jnp.where(lane < 16, high, 0.0)), off - 72)
        v = roll(jnp.where(jnp.logical_and(lane >= 16, lane < 88), high, 0.0), off - 16)
        for section, r in enumerate((q, k, v)):
            if off + HEAD_DIM > 128:
                pieces = [
                    (t, jnp.where(lane >= off, r, 0.0)), (t + 1, jnp.where(lane < off, r, 0.0))
                ]
            else:
                pieces = [(t, r)]
            for at, piece in pieces:
                old = tiles[section][at]
                tiles[section][at] = piece if old is None else old + piece
    for section in range(3):
        for t in range(GROUPS):
            at = section * D + t * 128
            dproj_b[:, at : at + 128] = tiles[section][t].astype(BF16)

    hidp[...] = jnp.zeros_like(hidp)

    def back1(c, carry):
        at = pl.ds(pl.multiple_of(c * D, 128), D)
        hidp[...] += dot_nt(dproj_b[:, at], wsp[:, at])
        return carry

    lax.fori_loop(0, 3, back1, 0)
    adj_rot1 = hidp[...].astype(BF16)
    packed = rotation_gradient(normed1[...].astype(BF16), adj_rot1)
    for g in range(GROUPS):
        for s in range(2):
            r2_snd[2 * g + s] = packed[g][16 * s : 16 * (s + 1)].astype(BF16)
    reduce_first(r2_snd, r2_rcv, 18, 10)
    adj_normed = rotate_transposed(adj_rot1, bd.at[0])
    wait_all(recv_sems.at[5], ah_rcv)
    grad = ah_rcv[...].reshape(TOKENS, D).astype(F32) + normalize_backward(
        adj_normed, normed1[...], inverse1[...]
    )
    vg_ref[...] = grad.astype(BF16).reshape(2, 64, D)
    reduce_second(r2_snd, r2_rcv, r2_z, 18, 10)
    reduce_third(r2_z, r2_chunk, r2_out, 18, 10)

    wait_all(send_sems.at[0], vid_mid.at[pl.ds(0, 6)])
    wait_all(send_sems.at[1], ct_mid.at[pl.ds(0, 6)])
    wait_all(send_sems.at[2], qkv_snd.at[pl.ds(0, PWAYS - 1)])
    wait_all(send_sems.at[3], att_snd.at[pl.ds(0, PATCHES - 16)])
    wait_all(send_sems.at[4], do_rcv.at[pl.ds(0, PATCHES - 16)])
    wait_all(send_sems.at[5], ah_snd.at[pl.ds(0, 6)])
    wait_all(send_sems.at[6], dq_snd.at[pl.ds(0, PATCHES - 64)])
    reduce_sent(r1_snd, r1_z, r1_out, 27, 7)
    wait_all(recv_sems.at[9], r1_out)
    red_ref[0 : 3 * ROWS] = r1_out[...].reshape(3 * ROWS, 128).astype(F32)
    reduce_sent(r2_snd, r2_z, r2_out, 18, 10)
    wait_all(recv_sems.at[12], r2_out)
    red_ref[3 * ROWS :] = r2_out[...].reshape(ROWS, 128).astype(F32)


def per_device(
    video,
    cotangent,
    frame_mask,
    spatial_project,
    spatial_output,
    temporal_project,
    temporal_output,
    spatial_inward,
    spatial_outward,
    temporal_inward,
    temporal_outward,
):
    vm = pltpu.VMEM
    scratch = [
        vm((D, 3 * D), BF16), vm((D, D), BF16), vm((D, 3 * D), BF16), vm((D, D), BF16),
        vm((4, D, BLOCK), F32), vm((4, D, 128), BF16),
        vm((2, 64, D), BF16), vm((2, 64, D), BF16), vm((FRAMES, 16, D), BF16), vm((FRAMES, 16, D), BF16),
        vm((TOKENS, D), F32), vm((TOKENS, 1), F32), vm((TOKENS, 3 * D + 128), F32),
        vm((PWAYS, 64, 256), BF16), vm((PATCHES, 256), BF16), vm((PATCHES, 128), BF16), vm((PATCHES, 128), BF16),
        vm((PATCHES, 128), BF16), vm((FRAMES, HEADS, 16, 128), BF16), vm((TOKENS, D), BF16),
        vm((TOKENS, D), F32), vm((TOKENS, D), BF16), vm((TOKENS, D + 128), BF16),
        vm((TOKENS, D), F32), vm((TOKENS, D), F32), vm((TOKENS, 3 * D + 128), BF16),
        vm((TOKENS, 3 * D + 128), F32), vm((TOKENS, D + 128), F32), vm((TOKENS, 3 * D), BF16),
        vm((FRAMES, 16, D), BF16), vm((2, 64, D), BF16),
        vm((FRAMES, HEADS, 16, 128), BF16), vm((PATCHES, 128), BF16),
        vm((PATCHES, 128), BF16), vm((PATCHES, 128), BF16),
        vm((PATCHES, 256), BF16), vm((PATCHES, 256), BF16),
        vm((128, PATCHES), BF16), vm((128, PATCHES), F32), vm((PATCHES, 256), F32),
        vm((PATCHES, 256), BF16), vm((PWAYS, 64, 256), BF16),
        vm((27, 32, 128), BF16), vm((PWAYS, 32, 128), BF16), vm((ZWAYS, 32, 128), F32),
        vm((32, 128), BF16), vm((27, 32, 128), BF16),
        vm((18, 16, 128), BF16), vm((PWAYS, 16, 128), BF16), vm((ZWAYS, 16, 128), F32),
        vm((16, 128), BF16), vm((18, 16, 128), BF16),
        pltpu.SemaphoreType.DMA((10,)), pltpu.SemaphoreType.DMA((1,)),
        pltpu.SemaphoreType.DMA((13,)), pltpu.SemaphoreType.DMA((13,)),
    ]
    anyspec = pl.BlockSpec(memory_space=pl.ANY)
    grad, red = pl.pallas_call(
        kernel,
        out_shape=(
            jax.ShapeDtypeStruct((2, 64, D), BF16),
            jax.ShapeDtypeStruct((4 * ROWS, 128), F32),
        ),
        in_specs=[pl.BlockSpec(memory_space=pltpu.SMEM)] + [anyspec] * 10,
        out_specs=(pl.BlockSpec(memory_space=pltpu.VMEM), pl.BlockSpec(memory_space=pltpu.VMEM)),
        scratch_shapes=scratch,
        compiler_params=pltpu.CompilerParams(
            collective_id=0, has_side_effects=True, vmem_limit_bytes=60 * 1024 * 1024
        ),
        name="block_backward",
    )(
        frame_mask, video, cotangent, spatial_project, spatial_output, temporal_project, temporal_output,
        *(r.reshape(D, BLOCK) for r in (spatial_inward, spatial_outward, temporal_inward, temporal_outward)),
    )
    red = red.reshape(4, GROUPS, BLOCK, 4, BLOCK).transpose(0, 1, 3, 2, 4).reshape(4, 36, BLOCK, BLOCK)
    sout, tin, tout, sin = red[0], red[1], red[2], red[3]
    return grad, sin, sout, tin, tout


def solution(mesh):
    split = P("frame", "patch", None)
    in_specs = (split, split) + (P(),) * 9
    out_specs = (split,) + (P(),) * 4
    return jax.shard_map(
        per_device, mesh=mesh, in_specs=in_specs, out_specs=out_specs, check_vma=False
    )
```

profile of v0, /device:TPU:1, one launch (start us, length us, event | category | flops | bytes accessed | tf_op | source)
XLA Modules:
  0.0 151.3 jit_solution(16666479977868154213)
XLA Ops:
  0.6 0.0 copy-start
  0.6 2.4 %copy.24 = f32[36,32,32]{2,1,0:T(8,128)} copy(f32[36,32,32]{0,2,1:T(8,128)} %param.18) | data formatting | bytes 294912 | tf_op args[7]
  3.1 2.4 %copy.25 = f32[36,32,32]{2,1,0:T(8,128)} copy(f32[36,32,32]{0,2,1:T(8,128)} %param.19) | data formatting | bytes 294912 | tf_op args[8]
  5.4 2.4 %copy.26 = f32[36,32,32]{2,1,0:T(8,128)} copy(f32[36,32,32]{0,2,1:T(8,128)} %param.20) | data formatting | bytes 294912 | tf_op args[9]
  7.8 0.0 copy-done
  7.8 1.3 copy.27
  9.2 133.7 %block_backward.1 = (bf16[2,64,1152]{2,1,0:T(8,128)(2,1)}, f32[1152,128]{1,0:T(8,128)}) custom-call(s32[8]{0:T(128)} %mask_ref.1, bf16[2,64,1152]{2,1,0:T(8,128)(2,1)} %video.1, bf16[2,64,1152]{2,1,0:T(8,128)(2,1)} %cotangent.1, bf16[1152,3456]{1,0:T(8,128)(2,1)} %wsp_h.1, bf16[1152,1152]{1,0:T(8,128)(2,1)} %wso_h.1, bf16[1152,3456]{1,0:T(8,128)(2,1)} %wtp_h.1, ...), custom_call_target="tpu_custom_call" | custom-call | tf_op jit(solution)/shard_map/block_backward/pallas_call | solution.py:641
  142.9 2.2 %reshape.38 = f32[4,9,32,4,32]{4,3,2,1,0:T(4,128)S(1)} reshape(f32[1152,128]{1,0:T(8,128)} %get-tuple-element.8) | data formatting | bytes 1179648 | tf_op jit(solution)/shard_map/reshape | solution.py:658
  145.0 0.3 copy.34
  145.3 0.3 fusion
  145.7 0.0 copy-start.1
  145.7 1.2 copy.32
  146.9 1.2 copy.31
  148.1 1.2 copy.30
  149.4 1.2 copy.29
  150.6 0.0 copy-done.1
  150.6 0.7 copy.36
Async XLA Ops:
  0.6 7.2 %copy-start = (f32[36,32,32]{0,2,1:T(8,128)S(1)}, f32[36,32,32]{0,2,1:T(8,128)}, u32[]{:S(2)}) copy-start(f32[36,32,32]{0,2,1:T(8,128)} %param.21) | copy-start | bytes 442372
  145.7 5.0 %copy-start.1 = (bf16[2,64,1152]{2,1,0:T(8,128)(2,1)S(1)}, bf16[2,64,1152]{2,1,0:T(8,128)(2,1)}, u32[]{:S(2)}) copy-start(bf16[2,64,1152]{2,1,0:T(8,128)(2,1)} %get-tuple-element.23) | copy-start | bytes 884740
where the time goes:
time: 152 us; the launch traced here: 151 us
  Pallas kernels  134 us (88%)
  local copies, waits for them, and re-layouts  17 us (11%)
    pallas_call x1, Pallas kernels, per_device(): pl.pallas_call(kernel, out_shape=(jax.ShapeDtypeStruct((2, 64, D), BF16),...  134 us
    unnamed x13, local copies, waits for them, and re-layouts  14.2 us

commit v1 on v0

v1 whole, which is shorter than its diff:
```python
import itertools
import math

import jax
import jax.numpy as jnp
from jax import lax
from jax.experimental import pallas as pl
from jax.experimental.pallas import tpu as pltpu
from jax.sharding import PartitionSpec as P

D = 1152
HEADS = 16
HEAD_DIM = 72
BLOCK = 32
GROUPS = D // 128
FRAMES = 8
PATCHES = 2048
ZWAYS = 4
PWAYS = 32
DEVICES = ZWAYS * PWAYS
TOKENS = 128
ROWS = D // 4
NBLOCK = D // 32

EPSILON = 1e-06
NEGATIVE = -1e30
SCALE = 1.0 / math.sqrt(HEAD_DIM)
LOG2E = math.log2(math.e)
LN2 = math.log(2.0)

F32 = jnp.float32
BF16 = jnp.bfloat16
MESH = pl.DeviceIdType.MESH


def hops(step):
    return min(step[0], 4 - step[0]) + min(step[1], 4 - step[1]) + min(step[3], 4 - step[3])


PLANE = sorted(
    [s for s in itertools.product(range(4), range(4), range(2), [0]) if any(s)], key=lambda s: -hops(s)
)
SPACE = sorted(
    [s for s in itertools.product(range(4), range(4), range(2), range(4)) if any(s)],
    key=lambda s: -hops(s),
)
SLOTS = PLANE + [(0, 0, 0, 0)]
SLOT_OF = {s[:3]: n for n, s in enumerate(SLOTS)}


def dot(a, b):
    return lax.dot_general(a, b, (((1,), (0,)), ((), ())), preferred_element_type=F32)


def dot_nt(a, b):
    return lax.dot_general(a, b, (((1,), (1,)), ((), ())), preferred_element_type=F32)


def dot_tn(a, b):
    return lax.dot_general(a, b, (((0,), (0,)), ((), ())), preferred_element_type=F32)


def lanes(shape):
    return lax.broadcasted_iota(jnp.int32, shape, len(shape) - 1)


def rows(shape):
    return lax.broadcasted_iota(jnp.int32, shape, 0)


def roll(x, amount):
    amount = amount % 128
    return x if amount == 0 else pltpu.roll(x, amount, 1)


def normalize(x):
    centered = x - jnp.mean(x, axis=-1, keepdims=True)
    inverse = lax.rsqrt(jnp.mean(centered * centered, axis=-1, keepdims=True) + EPSILON)
    return centered * inverse, inverse


def normalize_backward(adjoint, normed, inverse):
    grad_mean = jnp.mean(adjoint, axis=-1, keepdims=True)
    grad_cross = jnp.mean(adjoint * normed, axis=-1, keepdims=True)
    return inverse * (adjoint - grad_mean - normed * grad_cross)


def group(x, g):
    return x[:, g * 128 : (g + 1) * 128]


def rotate(x, blocks):
    return jnp.concatenate(
        [dot(group(x, g), blocks[g * 128 : (g + 1) * 128, :]) for g in range(GROUPS)], axis=1
    )


def rotate_transposed(x, blocks):
    return jnp.concatenate(
        [dot_nt(group(x, g), blocks[g * 128 : (g + 1) * 128, :]) for g in range(GROUPS)], axis=1
    )


def block_mask(shape):
    return (rows(shape) // BLOCK) % 4 == lanes(shape) // BLOCK


def rotation_gradient(left, right):
    mask = block_mask((128, 128))
    packed = []
    for g in range(GROUPS):
        full = jnp.where(mask, dot_tn(group(left, g), group(right, g)), 0.0)
        packed.append(full[0:32] + full[32:64] + full[64:96] + full[96:128])
    return packed


def kernel(
    mask_ref, video, cotangent, wsp_h, wso_h, wtp_h, wto_h, rsi_h, rso_h, rti_h, rto_h,
    vg_ref, red_ref,
    wsp, wso, wtp, wto, r4, bd32, bd,
    vid, cot, vid_mid, ct_mid,
    normed1, inverse1, rot_b, proj,
    qkv_snd, qkv_rcv, kx, qx, vx,
    att_snd, att_rcv, att1, top, aot, daz,
    hidp, normed2, proj2, att2_b, dproj_b,
    t_s, t_dp, t_p, t_ds,
    ah_snd, ah_rcv, do_snd, do_rcv, dox, dosh, qsh, kt, dqt, pt,
    dkv_snd, dkv_rcv, dq_snd, dq_rcv, vg,
    r1_snd, r1_rcv, r1_z, r1_chunk, r1_out,
    r2_snd, r2_rcv, r2_z, r2_chunk, r2_out,
    load_sems, out_sems, send_sems, recv_sems, qkv_sems,
):
    z = lax.axis_index("frame")
    j = lax.axis_index("patch")
    px, py, pc = j >> 3, (j >> 1) & 3, j & 1
    xs = [((px + d) & 3) * 8 for d in range(4)]
    ys = [((py + d) & 3) * 2 for d in range(4)]
    cs = [(pc + d) & 1 for d in range(2)]
    zs = [(z + d) & 3 for d in range(4)]
    xys = [[a + b for b in ys] for a in xs]

    def ahead(step):
        return zs[step[3]], xys[step[0]][step[1]] + cs[step[2]]

    def behind(step):
        return zs[-step[3] & 3], xys[-step[0] & 3][-step[1] & 3] + cs[step[2]]

    def load(src, dst, n):
        return pltpu.make_async_copy(src, dst, load_sems.at[n])

    early = [load(video, vid, 0), load(rsi_h, r4.at[0], 1), load(wsp_h, wsp, 2)]
    late = [
        load(cotangent, cot, 3), load(rso_h, r4.at[1], 4), load(rti_h, r4.at[2], 5),
        load(rto_h, r4.at[3], 6), load(wto_h, wto, 7), load(wso_h, wso, 8), load(wtp_h, wtp, 9),
    ]
    for copy in early:
        copy.start()

    barrier = pltpu.get_barrier_semaphore()
    for step in SPACE:
        pl.semaphore_signal(barrier, inc=1, device_id=ahead(step), device_id_type=MESH)

    def local(src, dst, sem):
        pltpu.make_async_copy(src, dst, sem).start()

    def remote(src, dst, phase, there, recv_sem=None):
        pltpu.make_async_remote_copy(
            src_ref=src, dst_ref=dst, send_sem=send_sems.at[phase],
            recv_sem=recv_sems.at[phase] if recv_sem is None else recv_sem,
            device_id=there, device_id_type=MESH,
        ).start()

    def wait_all(sem, buffer):
        pltpu.make_async_copy(buffer, buffer, sem).wait()

    def make_blocks(index):
        shape = (128, 512)
        spread = jnp.where(
            jnp.logical_and(
                rows(shape) // BLOCK == lanes(shape) // 128, rows(shape) % BLOCK == lanes(shape) % BLOCK
            ),
            1.0, 0.0,
        ).astype(BF16)
        shape = (NBLOCK, 128)
        own = rows(shape) % 4 == lanes(shape) // BLOCK
        for m in range(8):
            four = r4[index, 4 * m : 4 * m + 4].reshape(128, NBLOCK).astype(BF16)
            wide = dot_tn(four, spread)
            for s in range(4):
                bd32[pl.ds(4 * m + s, NBLOCK, stride=BLOCK), :] = jnp.where(own, group(wide, s), 0.0)
        bd[index] = bd32[...].astype(BF16)

    early[0].wait()
    normed, inverse = normalize(vid[...].reshape(TOKENS, D).astype(F32))
    normed1[...] = normed
    inverse1[...] = inverse
    early[1].wait()
    make_blocks(0)
    rot_b[...] = rotate(normed1[...].astype(BF16), bd.at[0]).astype(BF16)

    early[2].wait()
    for copy in late:
        copy.start()

    def project1(c, carry):
        at = pl.ds(pl.multiple_of(c * D, 128), D)
        proj[:, at] = dot(rot_b[...], wsp[:, at])
        return carry

    lax.fori_loop(0, 3, project1, 0)

    lane = lanes((TOKENS, 128))
    qscale = jnp.where(lane < HEAD_DIM, SCALE * LOG2E, 1.0)
    for h in range(HEADS):
        t, off = (HEAD_DIM * h) // 128, (HEAD_DIM * h) % 128

        def pick(section, to):
            first = proj[:, section * D + t * 128 : section * D + (t + 1) * 128]
            if off + HEAD_DIM > 128:
                second = proj[:, section * D + (t + 1) * 128 : section * D + (t + 2) * 128]
                first = jnp.where(lane >= off, first, second)
            return roll(first, to - off)

        q, k, v = pick(0, 0), pick(1, 72), pick(2, 16)
        low = (jnp.where(lane < 72, q, k) * qscale).astype(BF16)
        high = jnp.where(lane < 16, k, jnp.where(lane < 88, v, 0.0)).astype(BF16)
        for f in range(2):
            qkv_snd[f * HEADS + h, :, 0:128] = low[64 * f : 64 * (f + 1)]
            qkv_snd[f * HEADS + h, :, 128:256] = high[64 * f : 64 * (f + 1)]

    pl.semaphore_wait(barrier, DEVICES - 1)

    for n, step in enumerate(SLOTS):
        dst = qkv_rcv.at[pl.ds(64 * n, 64)]
        if any(step):
            zz, jj = ahead(step)
            remote(qkv_snd.at[jj], dst, 2, (zz, jj), qkv_sems.at[n // 8])
        else:
            local(qkv_snd.at[j], dst, qkv_sems.at[n // 8])

    late[0].wait()
    for phase, src, dst in ((1, cot, ct_mid), (0, vid, vid_mid)):
        for d in (2, 1, 3, 0):
            for f in range(2):
                piece = src.at[f, pl.ds(pl.multiple_of(zs[d] * 16, 16), 16)]
                if d:
                    remote(piece, dst.at[2 * z + f], phase, (zs[d], j))
                else:
                    local(piece, dst.at[2 * z + f], recv_sems.at[phase])

    for n in (1, 2, 3):
        late[n].wait()
        make_blocks(n)

    wait_all(recv_sems.at[1], ct_mid)
    frame_row = rows((TOKENS, 1)) // 16
    valid = jnp.zeros((TOKENS, 1), F32)
    for f in range(FRAMES):
        valid = jnp.where(frame_row == f, mask_ref[f].astype(F32), valid)
    top[...] = ct_mid[...].reshape(TOKENS, D).astype(F32) * valid
    late[4].wait()
    aot[...] = dot_nt(top[...].astype(BF16), wto[...]).astype(BF16)
    daz[:, 0:D] = rotate_transposed(aot[...], bd.at[3]).astype(BF16)
    daz[:, D:] = jnp.zeros((TOKENS, 128), BF16)

    lane2 = lanes((256, 128))
    ones = jnp.where(jnp.logical_and(lane2 >= 72, lane2 < 76), 1.0, 0.0)

    def prepare(i, carry):
        at = pl.ds(pl.multiple_of(i * 256, 256), 256)
        t0, t1 = qkv_rcv[at, 0:128].astype(F32), qkv_rcv[at, 128:256].astype(F32)
        k = roll(jnp.where(lane2 >= 72, t0, t1), -72)
        kx[at, :] = jnp.where(lane2 < 72, k, ones).astype(BF16)
        vx[at, :] = jnp.where(lane2 < 72, roll(t1, -16), ones).astype(BF16)
        qx[at, :] = jnp.where(lane2 < 72, t0, 0.0).astype(BF16)
        return carry

    for g in range(4):
        wait_all(qkv_sems.at[g], qkv_rcv.at[pl.ds(512 * g, 512)])
        lax.fori_loop(2 * g, 2 * g + 2, prepare, 0)

    def attend(i, carry):
        spans = [pl.ds(pl.multiple_of(i * 512 + s * 256, 256), 256) for s in range(2)]
        outs = []
        for at in spans:
            scores = dot_nt(qx[at, :], kx[...])
            high_score = jnp.max(scores, axis=-1, keepdims=True)
            outs.append((high_score, dot(jnp.exp2(scores - high_score).astype(BF16), vx[...])))
        for at, (high_score, out) in zip(spans, outs):
            total = out[:, 72:73]
            att_snd[at, :] = jnp.where(lane2 < 72, out / total, 0.0).astype(BF16)
            neg = -(high_score + jnp.log(total) * LOG2E)
            hi = neg.astype(BF16).astype(F32)
            mid = (neg - hi).astype(BF16).astype(F32)
            lo = neg - hi - mid
            old = qx[at, :].astype(F32)
            new = jnp.where(
                lane2 == 72, hi, jnp.where(lane2 == 73, mid, jnp.where(lane2 == 74, lo, old))
            )
            qx[at, :] = new.astype(BF16)

        for ii in range(4):

            @pl.when(i == ii)
            def _():
                for n in range(8 * ii, 8 * ii + 8):
                    for d in (2, 1, 3, 0):
                        zz, jj = zs[d], behind(SLOTS[n])[1]
                        src = att_snd.at[pl.ds(pl.multiple_of(64 * n + 16 * zz, 16), 16)]
                        dst = att_rcv.at[2 * z + (j >> 4), j & 15]
                        if d or any(SLOTS[n]):
                            remote(src, dst, 3, (zz, jj))
                        else:
                            local(src, dst, recv_sems.at[3])

        return carry

    lax.fori_loop(0, 4, attend, 0)

    wait_all(recv_sems.at[0], vid_mid)
    wait_all(recv_sems.at[3], att_rcv)

    def add_piece(tiles, at, piece):
        tiles[at] = piece if tiles[at] is None else tiles[at] + piece

    def place(tiles, h, value):
        t, off = (HEAD_DIM * h) // 128, (HEAD_DIM * h) % 128
        if off + HEAD_DIM > 128:
            add_piece(tiles, t, jnp.where(lane >= off, value, 0.0))
            add_piece(tiles, t + 1, jnp.where(lane < off, value, 0.0))
        else:
            add_piece(tiles, t, value)

    tiles = [None] * GROUPS
    for h in range(HEADS):
        place(tiles, h, roll(att_rcv[:, h].reshape(TOKENS, 128).astype(F32), (HEAD_DIM * h) % 128))
    for t in range(GROUPS):
        att1[:, t * 128 : (t + 1) * 128] = tiles[t].astype(BF16)

    late[5].wait()
    outrot = rotate(att1[...], bd.at[1]).astype(BF16)
    hidden = vid_mid[...].reshape(TOKENS, D).astype(F32) + dot(outrot, wso[...])
    hidden = hidden.astype(BF16).astype(F32)
    normed, inverse2 = normalize(hidden)
    normed2[...] = normed
    rot_b[...] = rotate(normed.astype(BF16), bd.at[2]).astype(BF16)
    late[6].wait()

    def project2(c, carry):
        at = pl.ds(pl.multiple_of(c * D, 128), D)
        proj2[:, at] = dot(rot_b[...], wtp[:, at]).astype(BF16)
        return carry

    lax.fori_loop(0, 3, project2, 0)

    square = (TOKENS, TOKENS)
    same_patch = rows(square) % 16 == lanes(square) % 16
    same_frame = rows(square) // 16 == lanes(square) // 16
    key_valid = jnp.zeros(square, F32)
    for f in range(FRAMES):
        key_valid = jnp.where(rows(square) // 16 == f, mask_ref[f].astype(F32), key_valid)
    allowed = jnp.logical_and(same_patch, jnp.logical_or(key_valid == 1.0, same_frame))
    bias = jnp.where(allowed, 0.0, NEGATIVE)

    def window(h, section):
        t, off = (HEAD_DIM * h) // 128, (HEAD_DIM * h) % 128
        width = 256 if off + HEAD_DIM > 128 else 128
        return slice(section * D + t * 128, section * D + t * 128 + width)

    def own_lanes(h):
        off = (HEAD_DIM * h) % 128
        l = lanes((1, 256 if off + HEAD_DIM > 128 else 128))
        return jnp.where(jnp.logical_and(l >= off, l < off + HEAD_DIM), 1.0, 0.0)

    for h in range(HEADS):
        own = own_lanes(h).astype(BF16)
        t_s[h] = dot_nt(proj2[:, window(h, 1)], proj2[:, window(h, 0)] * own)
        t_dp[h] = dot_nt(proj2[:, window(h, 2)], daz[:, window(h, 0)] * own)

    for h in range(HEADS):
        scores = t_s[h] * SCALE + bias
        e = jnp.exp(scores - jnp.max(scores, axis=0, keepdims=True))
        p = e * (1.0 / jnp.sum(e, axis=0, keepdims=True))
        dp = t_dp[h]
        t_p[h] = p.astype(BF16)
        t_ds[h] = (p * (dp - jnp.sum(p * dp, axis=0, keepdims=True))).astype(BF16)

    def gather(section, dst, base):
        tiles = [None] * (GROUPS + 1)
        for h in range(HEADS):
            own = own_lanes(h)
            own_b = own.astype(BF16)
            if section == 0:
                part = dot_tn(t_ds[h], proj2[:, window(h, 1)]) * (own * SCALE)
            elif section == 1:
                part = dot(t_ds[h], proj2[:, window(h, 0)] * own_b) * SCALE
            elif section == 2:
                part = dot(t_p[h], daz[:, window(h, 0)] * own_b)
            else:
                part = dot_tn(t_p[h], proj2[:, window(h, 2)]) * own
            t = (HEAD_DIM * h) // 128
            for w in range(part.shape[1] // 128):
                add_piece(tiles, t + w, group(part, w))
        for t in range(GROUPS):
            dst[:, base + t * 128 : base + (t + 1) * 128] = tiles[t].astype(BF16)

    for section in range(3):
        gather(section, dproj_b, section * D)

    hidp[...] = jnp.zeros_like(hidp)

    def back2(c, carry):
        at = pl.ds(pl.multiple_of(c * D, 128), D)
        hidp[...] += dot_nt(dproj_b[:, at], wtp[:, at])
        return carry

    lax.fori_loop(0, 3, back2, 0)
    adj_rot2 = hidp[...].astype(BF16)
    adj_normed = rotate_transposed(adj_rot2, bd.at[2])
    adj_hidden = top[...] + normalize_backward(adj_normed, normed2[...], inverse2)
    adj_hidden_b = adj_hidden.astype(BF16)
    ah_snd[...] = adj_hidden_b.reshape(FRAMES, 16, D)
    aho = dot_nt(adj_hidden_b, wso[...]).astype(BF16)
    adj_att1 = rotate_transposed(aho, bd.at[1])
    for h in range(HEADS):
        t, off = (HEAD_DIM * h) // 128, (HEAD_DIM * h) % 128
        first = group(adj_att1, t)
        if off + HEAD_DIM > 128:
            first = jnp.where(lane >= off, first, group(adj_att1, t + 1))
        piece = jnp.where(lane < 72, roll(first, -off), 0.0).astype(BF16)
        do_snd[:, h] = piece.reshape(FRAMES, 16, 128)

    for step in SPACE + [(0, 0, 0, 0)]:
        zz, jj = ahead(step)
        src = do_snd.at[2 * zz + (jj >> 4), jj & 15]
        dst = do_rcv.at[pl.ds(pl.multiple_of(64 * SLOT_OF[step[:3]] + 16 * z, 16), 16)]
        if any(step):
            remote(src, dst, 4, (zz, jj))
        else:
            local(src, dst, recv_sems.at[4])
    for d in (2, 1, 3, 0):
        for f in range(2):
            src = ah_snd.at[2 * zs[d] + f]
            dst = ah_rcv.at[f, pl.ds(pl.multiple_of(z * 16, 16), 16)]
            if d:
                remote(src, dst, 5, (zs[d], j))
            else:
                local(src, dst, recv_sems.at[5])

    gather(3, att2_b, 0)
    for n, packed in enumerate((
        rotation_gradient(att1[...], aho),
        rotation_gradient(normed2[...].astype(BF16), adj_rot2),
        rotation_gradient(att2_b[...], aot[...]),
    )):
        for g in range(GROUPS):
            r1_snd[n * GROUPS + g] = packed[g].astype(BF16)

    def reduce_first(snd, rcv, chunk_of, owns, phase):
        for step in SLOTS:
            zz, jj = ahead(step)

            @pl.when(owns(jj))
            def _():
                if any(step):
                    remote(snd.at[chunk_of(jj)], rcv.at[j], phase, (zz, jj))
                else:
                    local(snd.at[chunk_of(jj)], rcv.at[j], recv_sems.at[phase])

    def reduce_second(rcv, zbuf, owns, phase):
        @pl.when(owns(j))
        def _():
            wait_all(recv_sems.at[phase], rcv)
            zbuf[z] = jnp.sum(rcv[...].astype(F32), axis=0)
            for d in (2, 1, 3):
                remote(zbuf.at[z], zbuf.at[z], phase + 1, (zs[d], j))

    def reduce_third(zbuf, chunk, out, chunk_of, owns, phase):
        size = chunk.shape[0]

        @pl.when(owns(j))
        def _():
            wait_all(recv_sems.at[phase + 1], zbuf.at[pl.ds(0, ZWAYS - 1)])
            chunk[...] = (((zbuf[0] + zbuf[1]) + (zbuf[2] + zbuf[3])) / 128.0).astype(BF16)
            dst = out.at[pl.ds(pl.multiple_of(chunk_of(j) * size, size), size)]
            for step in SLOTS:
                if any(step):
                    remote(chunk, dst, phase + 2, ahead(step))
                else:
                    local(chunk, dst, recv_sems.at[phase + 2])

    def reduce_sent(snd, rcv, zbuf, owners, owns, phase):
        @pl.when(owns(j))
        def _():
            wait_all(send_sems.at[phase], snd.at[pl.ds(0, owners - 1)])
            wait_all(send_sems.at[phase + 1], zbuf.at[pl.ds(0, ZWAYS - 1)])
            wait_all(send_sems.at[phase + 2], rcv.at[pl.ds(0, PWAYS - 1)])

        @pl.when(jnp.logical_not(owns(j)))
        def _():
            wait_all(send_sems.at[phase], snd)

    def chunk1(jj):
        return jj

    def owns1(jj):
        return jj < 27

    def chunk2(jj):
        return jnp.where((jj & 1) == 0, jj >> 1, 16 + (jj >> 4))

    def owns2(jj):
        return jnp.logical_or((jj & 1) == 0, (jj & 15) == 1)

    reduce_first(r1_snd, r1_rcv, chunk1, owns1, 7)

    def probabilities(i, carry):
        for s in range(2):
            at = pl.ds(pl.multiple_of(i * 512 + s * 256, 256), 256)
            pt[at, :] = jnp.exp2(dot_nt(kx[at, :], qx[...])).astype(BF16)
        return carry

    lax.fori_loop(0, 4, probabilities, 0)

    def prepare_keys(i, carry):
        at = pl.ds(pl.multiple_of(i * 256, 256), 256)
        kt[:, at] = kx[at, :].astype(F32).T.astype(BF16)
        qsh[at, :] = jnp.where(lane2 < 72, qx[at, :].astype(F32), 0.0).astype(BF16)
        return carry

    lax.fori_loop(0, 8, prepare_keys, 0)
    wait_all(recv_sems.at[4], do_rcv)

    def prepare_back(i, carry):
        at = pl.ds(pl.multiple_of(i * 256, 256), 256)
        g = do_rcv[at, :].astype(F32)
        delta = -jnp.sum(g * att_snd[at, :].astype(F32), axis=-1, keepdims=True)
        hi = delta.astype(BF16).astype(F32)
        lo = delta - hi
        dox[at, :] = jnp.where(lane2 == 72, hi, jnp.where(lane2 == 73, lo, g)).astype(BF16)
        g = roll(g, 72)
        dosh[at, 0:128] = jnp.where(lane2 >= 72, g, 0.0).astype(BF16)
        dosh[at, 128:256] = jnp.where(lane2 < 16, g, 0.0).astype(BF16)
        return carry

    lax.fori_loop(0, 8, prepare_back, 0)
    dqt[...] = jnp.zeros_like(dqt)

    def attend_back(i, carry):
        update = None
        for s in range(2):
            at = pl.ds(pl.multiple_of(i * 512 + s * 256, 256), 256)
            p = pt[at, :]
            ds = (p.astype(F32) * dot_nt(vx[at, :], dox[...])).astype(BF16)
            part = dot(kt[:, at], ds)
            update = part if update is None else update + part
            dv = dot(p, dosh[...])
            dk = dot(ds, qsh[...]) * LN2
            low = (dv[:, 0:128] + dk).astype(BF16)
            for m in range(4):
                tail = dv[64 * m : 64 * m + 8, 128:256]
                for e in range(1, 8):
                    tail = tail + roll(dv[64 * m + 8 * e : 64 * m + 8 * e + 8, 128:256], 16 * e)
                slot = i * 8 + s * 4 + m
                dkv_snd[slot, 0:64] = low[64 * m : 64 * m + 64]
                dkv_snd[slot, 64:80] = jnp.concatenate([tail, jnp.zeros_like(tail)], axis=0).astype(BF16)
        dqt[...] += update

        for ii in range(4):

            @pl.when(i == ii)
            def _():
                for n in range(8 * ii, 8 * ii + 8):
                    there = behind(SLOTS[n])
                    if any(SLOTS[n]):
                        remote(dkv_snd.at[n], dkv_rcv.at[j], 6, there)
                    else:
                        local(dkv_snd.at[n], dkv_rcv.at[j], recv_sems.at[6])

        return carry

    lax.fori_loop(0, 4, attend_back, 0)

    def finish_back(i, carry):
        at = pl.ds(pl.multiple_of(i * 512, 512), 512)
        dq_snd[at, :] = (dqt[:, at].T * SCALE).astype(BF16)
        for ii in range(4):

            @pl.when(i == ii)
            def _():
                for n in range(8 * ii, 8 * ii + 8):
                    there = behind(SLOTS[n])
                    src = dq_snd.at[pl.ds(64 * n, 64)]
                    if any(SLOTS[n]):
                        remote(src, dq_rcv.at[j], 13, there)
                    else:
                        local(src, dq_rcv.at[j], recv_sems.at[13])

        return carry

    lax.fori_loop(0, 4, finish_back, 0)
    reduce_second(r1_rcv, r1_z, owns1, 7)
    wait_all(recv_sems.at[6], dkv_rcv)

    def both(buffer, h, part):
        return jnp.concatenate([buffer[h, part], buffer[HEADS + h, part]], axis=0).astype(F32)

    tiles_k, tiles_v = [None] * GROUPS, [None] * GROUPS
    for h in range(HEADS):
        off = (HEAD_DIM * h) % 128
        low = both(dkv_rcv, h, slice(0, 64))
        tails = []
        for f in range(2):
            tail = dkv_rcv[f * HEADS + h, 64:80].astype(F32)[0:8]
            tails += [roll(tail, -16 * e) for e in range(8)]
        tail = jnp.concatenate(tails, axis=0)
        place(tiles_k, h, roll(jnp.where(lane < 72, low, 0.0), off))
        v = jnp.where(lane >= 72, low, jnp.where(lane < 16, tail, 0.0))
        place(tiles_v, h, roll(v, off - 72))
    for t in range(GROUPS):
        dproj_b[:, D + t * 128 : D + (t + 1) * 128] = tiles_k[t].astype(BF16)
        dproj_b[:, 2 * D + t * 128 : 2 * D + (t + 1) * 128] = tiles_v[t].astype(BF16)
    hidp[...] = jnp.zeros_like(hidp)

    def back1(c, carry):
        at = pl.ds(pl.multiple_of(c * D, 128), D)
        hidp[...] += dot_nt(dproj_b[:, at], wsp[:, at])
        return carry

    lax.fori_loop(1, 3, back1, 0)
    reduce_third(r1_z, r1_chunk, r1_out, chunk1, owns1, 7)
    wait_all(recv_sems.at[13], dq_rcv)
    tiles = [None] * GROUPS
    for h in range(HEADS):
        low = jnp.where(lane < 72, both(dq_rcv, h, slice(0, 64)), 0.0)
        place(tiles, h, roll(low, (HEAD_DIM * h) % 128))
    for t in range(GROUPS):
        dproj_b[:, t * 128 : (t + 1) * 128] = tiles[t].astype(BF16)
    lax.fori_loop(0, 1, back1, 0)
    adj_rot1 = hidp[...].astype(BF16)
    packed = rotation_gradient(normed1[...].astype(BF16), adj_rot1)
    for g in range(GROUPS):
        for s in range(2):
            r2_snd[2 * g + s] = packed[g][16 * s : 16 * (s + 1)].astype(BF16)
    reduce_first(r2_snd, r2_rcv, chunk2, owns2, 10)
    adj_normed = rotate_transposed(adj_rot1, bd.at[0])
    wait_all(recv_sems.at[5], ah_rcv)
    grad = ah_rcv[...].reshape(TOKENS, D).astype(F32) + normalize_backward(
        adj_normed, normed1[...], inverse1[...]
    )
    vg[...] = grad.astype(BF16).reshape(2, 64, D)
    vg_out = pltpu.make_async_copy(vg, vg_ref, out_sems.at[0])
    vg_out.start()
    reduce_second(r2_rcv, r2_z, owns2, 10)
    wait_all(send_sems.at[0], vid_mid.at[pl.ds(0, 6)])
    wait_all(send_sems.at[1], ct_mid.at[pl.ds(0, 6)])
    wait_all(send_sems.at[2], qkv_snd.at[pl.ds(0, PWAYS - 1)])
    wait_all(send_sems.at[3], att_snd.at[pl.ds(0, PATCHES - 16)])
    wait_all(send_sems.at[4], do_rcv.at[pl.ds(0, PATCHES - 16)])
    wait_all(send_sems.at[5], ah_snd.at[pl.ds(0, 6)])
    wait_all(send_sems.at[6], dkv_snd.at[pl.ds(0, PWAYS - 1)])
    wait_all(send_sems.at[13], dq_snd.at[pl.ds(0, PATCHES - 64)])
    wait_all(recv_sems.at[9], r1_out)
    red1 = pltpu.make_async_copy(r1_out, red_ref.at[pl.ds(0, 3 * ROWS)], out_sems.at[1])
    red1.start()
    reduce_third(r2_z, r2_chunk, r2_out, chunk2, owns2, 10)
    reduce_sent(r1_snd, r1_rcv, r1_z, 27, owns1, 7)
    reduce_sent(r2_snd, r2_rcv, r2_z, 18, owns2, 10)
    wait_all(recv_sems.at[12], r2_out)
    red2 = pltpu.make_async_copy(r2_out, red_ref.at[pl.ds(3 * ROWS, ROWS)], out_sems.at[2])
    red2.start()
    red1.wait()
    vg_out.wait()
    red2.wait()


def unpack_kernel(red, vg_in, vg_out, sout, tin, tout, sin, sem):
    copy = pltpu.make_async_copy(vg_in, vg_out, sem)
    copy.start()
    shape = (BLOCK, 40, ROWS)
    b = lax.broadcasted_iota(jnp.int32, shape, 0)
    n = lax.broadcasted_iota(jnp.int32, shape, 1)
    from_row = lax.broadcasted_iota(jnp.int32, shape, 2)
    pick = jnp.where(from_row == (n >> 2) * BLOCK + b, 1.0, 0.0).reshape(BLOCK * 40, ROWS).astype(BF16)
    shape = (BLOCK, 40, 128)
    n = lax.broadcasted_iota(jnp.int32, shape, 1)
    own = ((n & 3) == (lax.broadcasted_iota(jnp.int32, shape, 2) >> 5)).reshape(BLOCK * 40, 128)
    repeat = jnp.where(lanes((128, 128)) % BLOCK == rows((128, 128)) % BLOCK, 1.0, 0.0).astype(BF16)
    lane = lanes((40, 128)) >> 5
    for term, out in enumerate((sout, tin, tout, sin)):
        wide = dot(pick, red[term * ROWS : (term + 1) * ROWS, :])
        wide = dot(jnp.where(own, wide, 0.0).astype(BF16), repeat)
        for m in range(8):
            four = jnp.zeros((40, 128), F32)
            for s in range(4):
                at = (4 * m + s) * 40
                four = jnp.where(lane == s, wide[at : at + 40], four)
            out[4 * m : 4 * m + 4] = four.T[:, 0:NBLOCK].reshape(4, BLOCK, NBLOCK)
    copy.wait()


def per_device(
    video,
    cotangent,
    frame_mask,
    spatial_project,
    spatial_output,
    temporal_project,
    temporal_output,
    spatial_inward,
    spatial_outward,
    temporal_inward,
    temporal_outward,
):
    vm = pltpu.VMEM
    dma = pltpu.SemaphoreType.DMA
    scratch = [
        vm((D, 3 * D), BF16), vm((D, D), BF16), vm((D, 3 * D), BF16), vm((D, D), BF16),
        vm((4, BLOCK, BLOCK, NBLOCK), F32), vm((D, 128), F32), vm((4, D, 128), BF16),
        vm((2, 64, D), BF16), vm((2, 64, D), BF16), vm((FRAMES, 16, D), BF16), vm((FRAMES, 16, D), BF16),
        vm((TOKENS, D), F32), vm((TOKENS, 1), F32), vm((TOKENS, D), BF16), vm((TOKENS, 3 * D), F32),
        vm((PWAYS, 64, 256), BF16), vm((PATCHES, 256), BF16),
        vm((PATCHES, 128), BF16), vm((PATCHES, 128), BF16), vm((PATCHES, 128), BF16),
        vm((PATCHES, 128), BF16), vm((FRAMES, HEADS, 16, 128), BF16), vm((TOKENS, D), BF16),
        vm((TOKENS, D), F32), vm((TOKENS, D), BF16), vm((TOKENS, D + 128), BF16),
        vm((TOKENS, D), F32), vm((TOKENS, D), F32), vm((TOKENS, 3 * D), BF16),
        vm((TOKENS, D), BF16), vm((TOKENS, 3 * D), BF16),
        vm((HEADS, TOKENS, TOKENS), F32), vm((HEADS, TOKENS, TOKENS), F32),
        vm((HEADS, TOKENS, TOKENS), BF16), vm((HEADS, TOKENS, TOKENS), BF16),
        vm((FRAMES, 16, D), BF16), vm((2, 64, D), BF16),
        vm((FRAMES, HEADS, 16, 128), BF16), vm((PATCHES, 128), BF16),
        vm((PATCHES, 128), BF16), vm((PATCHES, 256), BF16), vm((PATCHES, 128), BF16),
        vm((128, PATCHES), BF16), vm((128, PATCHES), F32), vm((PATCHES, PATCHES), BF16),
        vm((PWAYS, 80, 128), BF16), vm((PWAYS, 80, 128), BF16),
        vm((PATCHES, 128), BF16), vm((PWAYS, 64, 128), BF16), vm((2, 64, D), BF16),
        vm((27, 32, 128), BF16), vm((PWAYS, 32, 128), BF16), vm((ZWAYS, 32, 128), F32),
        vm((32, 128), BF16), vm((3 * ROWS, 128), BF16),
        vm((18, 16, 128), BF16), vm((PWAYS, 16, 128), BF16), vm((ZWAYS, 16, 128), F32),
        vm((16, 128), BF16), vm((ROWS, 128), BF16),
        dma((10,)), dma((3,)), dma((14,)), dma((14,)), dma((4,)),
    ]
    anyspec = pl.BlockSpec(memory_space=pl.ANY)
    vspec = pl.BlockSpec(memory_space=pltpu.VMEM)
    blocks = [r.transpose(1, 2, 0) for r in (spatial_inward, spatial_outward, temporal_inward, temporal_outward)]
    grad, red = pl.pallas_call(
        kernel,
        out_shape=(
            jax.ShapeDtypeStruct((2, 64, D), BF16),
            jax.ShapeDtypeStruct((4 * ROWS, 128), BF16),
        ),
        in_specs=[pl.BlockSpec(memory_space=pltpu.SMEM)] + [anyspec] * 10,
        out_specs=(anyspec, anyspec),
        scratch_shapes=scratch,
        compiler_params=pltpu.CompilerParams(
            collective_id=0, has_side_effects=True, vmem_limit_bytes=62 * 1024 * 1024
        ),
        name="block_backward",
    )(
        frame_mask, video, cotangent, spatial_project, spatial_output, temporal_project, temporal_output,
        *blocks,
    )
    term = jax.ShapeDtypeStruct((BLOCK, BLOCK, NBLOCK), F32)
    grad, sout, tin, tout, sin = pl.pallas_call(
        unpack_kernel,
        out_shape=(jax.ShapeDtypeStruct((2, 64, D), BF16), term, term, term, term),
        in_specs=[vspec, anyspec],
        out_specs=(anyspec, vspec, vspec, vspec, vspec),
        scratch_shapes=[dma],
        compiler_params=pltpu.CompilerParams(vmem_limit_bytes=32 * 1024 * 1024),
        name="unpack_terms",
    )(red, grad)
    sin, sout, tin, tout = (r.transpose(2, 0, 1) for r in (sin, sout, tin, tout))
    return grad, sin, sout, tin, tout


def solution(mesh):
    split = P("frame", "patch", None)
    in_specs = (split, split) + (P(),) * 9
    out_specs = (split,) + (P(),) * 4
    return jax.shard_map(
        per_device, mesh=mesh, in_specs=in_specs, out_specs=out_specs, check_vma=False
    )
```

time: 152 us -> 102 us (0.67)
  Pallas kernels: 134 us -> 99.1 us
  local copies, waits for them, and re-layouts: 17 us -> 1.92 us
    pallas_call x1, Pallas kernels: 134 us -> 95.9 us  [per_device(): pl.pallas_call(kernel, out_shape=(jax.ShapeDtypeStruct((2, 64, D), BF16),...]
    unnamed x13 -> x4, local copies, waits for them, and re-layouts: 14.2 us -> 1.92 us
    pallas_call x0 -> x1, Pallas kernels: none -> 3.19 us  [per_device(): pl.pallas_call(unpack_kernel, out_shape=(jax.ShapeDtypeStruct((2, 64, D),...]
    reshape x2 -> x0, local copies, waits for them, and re-layouts: 2.47 us -> none  [per_device(): red.reshape(4, GROUPS, BLOCK, 4, BLOCK).transpose(0, 1, 3, 2, 4)]
where the time goes in v1:
time: 102 us
  Pallas kernels  99.1 us (97%)
  local copies, waits for them, and re-layouts  1.92 us (2%)
    pallas_call x1, Pallas kernels, per_device(): pl.pallas_call(kernel, out_shape=(jax.ShapeDtypeStruct((2, 64, D), BF16),...  95.9 us
    pallas_call x1, Pallas kernels, per_device(): pl.pallas_call(unpack_kernel, out_shape=(jax.ShapeDtypeStruct((2, 64, D),...  3.19 us

profile of v1, /device:TPU:1, one launch (start us, length us, event | category | flops | bytes accessed | tf_op | source)
XLA Modules:
  0.0 101.8 jit_solution(8323384703633692904)
XLA Ops:
  0.6 95.9 %block_backward.1 = (bf16[2,64,1152]{2,1,0:T(8,128)(2,1)}, bf16[1152,128]{1,0:T(8,128)(2,1)}) custom-call(s32[8]{0:T(128)} %mask_ref.1, bf16[2,64,1152]{2,1,0:T(8,128)(2,1)} %video.1, bf16[2,64,1152]{2,1,0:T(8,128)(2,1)} %cotangent.1, bf16[1152,3456]{1,0:T(8,128)(2,1)} %wsp_h.1, bf16[1152,1152]{1,0:T(8,128)(2,1)} %wso_h.1, bf16[1152,3456]{1,0:T(8,128)(2,1)} %wtp_h.1, ...), custom_call_target="tpu_custom_call" | custom-call | tf_op jit(solution)/shard_map/block_backward/pallas_call | solution.py:745
  96.5 0.0 copy-start
  96.5 1.0 copy-done
  97.5 0.0 copy-start.1
  97.5 1.0 copy-done.1
  98.4 3.2 %unpack_terms.1 = (bf16[2,64,1152]{2,1,0:T(8,128)(2,1)}, f32[32,32,36]{2,1,0:T(8,128)}, f32[32,32,36]{2,1,0:T(8,128)}, f32[32,32,36]{2,1,0:T(8,128)}, f32[32,32,36]{2,1,0:T(8,128)}) custom-call(bf16[1152,128]{1,0:T(8,128)(2,1)S(1)} %copy-done.1, bf16[2,64,1152]{2,1,0:T(8,128)(2,1)S(1)} %copy-done), custom_call_target="tpu_custom_call" | custom-call | tf_op jit(solution)/shard_map/unpack_terms/pallas_call | solution.py:763
Async XLA Ops:
  96.5 1.0 copy-start
  97.5 1.0 copy-start.1

commit v2 on v1

--- a/solution.py
+++ b/solution.py
@@ -124,11 +124,11 @@
     att_snd, att_rcv, att1, top, aot, daz,
     hidp, normed2, proj2, att2_b, dproj_b,
     t_s, t_dp, t_p, t_ds,
-    ah_snd, ah_rcv, do_snd, do_rcv, dox, dosh, qsh, kt, dqt, pt,
+    ah_snd, ah_rcv, do_snd, do_rcv, qt, dkt, dvt, pq,
     dkv_snd, dkv_rcv, dq_snd, dq_rcv, vg,
     r1_snd, r1_rcv, r1_z, r1_chunk, r1_out,
-    r2_snd, r2_rcv, r2_z, r2_chunk, r2_out,
-    load_sems, out_sems, send_sems, recv_sems, qkv_sems,
+    r2_snd, r2_rcv, r2_z, r2_chunk,
+    load_sems, out_sems, send_sems, recv_sems, qkv_sems, do_sems,
 ):
     z = lax.axis_index("frame")
     j = lax.axis_index("patch")
@@ -148,7 +148,10 @@
     def load(src, dst, n):
         return pltpu.make_async_copy(src, dst, load_sems.at[n])
 
-    early = [load(video, vid, 0), load(rsi_h, r4.at[0], 1), load(wsp_h, wsp, 2)]
+    early = [load(video, vid, 0), load(rsi_h, r4.at[0], 1)]
+    early += [
+        load(wsp_h.at[:, pl.ds(c * D, D)], wsp.at[:, pl.ds(c * D, D)], n) for c, n in enumerate((2, 10, 11))
+    ]
     late = [
         load(cotangent, cot, 3), load(rso_h, r4.at[1], 4), load(rti_h, r4.at[2], 5),
         load(rto_h, r4.at[3], 6), load(wto_h, wto, 7), load(wso_h, wso, 8), load(wtp_h, wtp, 9),
@@ -157,7 +160,8 @@
         copy.start()
 
     barrier = pltpu.get_barrier_semaphore()
-    for step in SPACE:
+    near = PLANE + [(0, 0, 0, d) for d in (2, 1, 3)]
+    for step in near:
         pl.semaphore_signal(barrier, inc=1, device_id=ahead(step), device_id_type=MESH)
 
     def local(src, dst, sem):
@@ -198,16 +202,12 @@
     make_blocks(0)
     rot_b[...] = rotate(normed1[...].astype(BF16), bd.at[0]).astype(BF16)
 
-    early[2].wait()
+    for c in range(3):
+        at = slice(c * D, (c + 1) * D)
+        early[2 + c].wait()
+        proj[:, at] = dot(rot_b[...], wsp[:, at])
     for copy in late:
         copy.start()
-
-    def project1(c, carry):
-        at = pl.ds(pl.multiple_of(c * D, 128), D)
-        proj[:, at] = dot(rot_b[...], wsp[:, at])
-        return carry
-
-    lax.fori_loop(0, 3, project1, 0)
 
     lane = lanes((TOKENS, 128))
     qscale = jnp.where(lane < HEAD_DIM, SCALE * LOG2E, 1.0)
@@ -228,7 +228,7 @@
             qkv_snd[f * HEADS + h, :, 0:128] = low[64 * f : 64 * (f + 1)]
             qkv_snd[f * HEADS + h, :, 128:256] = high[64 * f : 64 * (f + 1)]
 
-    pl.semaphore_wait(barrier, DEVICES - 1)
+    pl.semaphore_wait(barrier, len(near))
 
     for n, step in enumerate(SLOTS):
         dst = qkv_rcv.at[pl.ds(64 * n, 64)]
@@ -281,12 +281,14 @@
 
     def attend(i, carry):
         spans = [pl.ds(pl.multiple_of(i * 512 + s * 256, 256), 256) for s in range(2)]
-        outs = []
-        for at in spans:
+        highs = []
+        for s, at in enumerate(spans):
             scores = dot_nt(qx[at, :], kx[...])
-            high_score = jnp.max(scores, axis=-1, keepdims=True)
-            outs.append((high_score, dot(jnp.exp2(scores - high_score).astype(BF16), vx[...])))
-        for at, (high_score, out) in zip(spans, outs):
+            highs.append(jnp.max(scores, axis=-1, keepdims=True))
+            pq[256 * s : 256 * s + 256, :] = jnp.exp2(scores - highs[-1]).astype(BF16)
+        both_out = dot(pq[0:512, :], vx[...])
+        for s, (at, high_score) in enumerate(zip(spans, highs)):
+            out = both_out[256 * s : 256 * s + 256]
             total = out[:, 72:73]
             att_snd[at, :] = jnp.where(lane2 < 72, out / total, 0.0).astype(BF16)
             neg = -(high_score + jnp.log(total) * LOG2E)
@@ -407,14 +409,9 @@
     for section in range(3):
         gather(section, dproj_b, section * D)
 
-    hidp[...] = jnp.zeros_like(hidp)
-
-    def back2(c, carry):
-        at = pl.ds(pl.multiple_of(c * D, 128), D)
-        hidp[...] += dot_nt(dproj_b[:, at], wtp[:, at])
-        return carry
-
-    lax.fori_loop(0, 3, back2, 0)
+    for c in range(3):
+        at = slice(c * 384, (c + 1) * 384)
+        hidp[:, at] = dot_nt(dproj_b[...], wtp[at, :])
     adj_rot2 = hidp[...].astype(BF16)
     adj_normed = rotate_transposed(adj_rot2, bd.at[2])
     adj_hidden = top[...] + normalize_backward(adj_normed, normed2[...], inverse2)
@@ -433,11 +430,12 @@
     for step in SPACE + [(0, 0, 0, 0)]:
         zz, jj = ahead(step)
         src = do_snd.at[2 * zz + (jj >> 4), jj & 15]
-        dst = do_rcv.at[pl.ds(pl.multiple_of(64 * SLOT_OF[step[:3]] + 16 * z, 16), 16)]
+        n = SLOT_OF[step[:3]]
+        dst = do_rcv.at[pl.ds(pl.multiple_of(64 * n + 16 * z, 16), 16)]
         if any(step):
-            remote(src, dst, 4, (zz, jj))
+            remote(src, dst, 4, (zz, jj), do_sems.at[n // 8])
         else:
-            local(src, dst, recv_sems.at[4])
+            local(src, dst, do_sems.at[n // 8])
     for d in (2, 1, 3, 0):
         for f in range(2):
             src = ah_snd.at[2 * zs[d] + f]
@@ -506,143 +504,128 @@
     def owns1(jj):
         return jj < 27
 
-    def chunk2(jj):
-        return jnp.where((jj & 1) == 0, jj >> 1, 16 + (jj >> 4))
-
-    def owns2(jj):
-        return jnp.logical_or((jj & 1) == 0, (jj & 15) == 1)
-
     reduce_first(r1_snd, r1_rcv, chunk1, owns1, 7)
 
     def probabilities(i, carry):
         for s in range(2):
             at = pl.ds(pl.multiple_of(i * 512 + s * 256, 256), 256)
-            pt[at, :] = jnp.exp2(dot_nt(kx[at, :], qx[...])).astype(BF16)
+            pq[at, :] = jnp.exp2(dot_nt(qx[at, :], kx[...])).astype(BF16)
         return carry
 
     lax.fori_loop(0, 4, probabilities, 0)
 
-    def prepare_keys(i, carry):
+    def prepare_queries(i, carry):
         at = pl.ds(pl.multiple_of(i * 256, 256), 256)
-        kt[:, at] = kx[at, :].astype(F32).T.astype(BF16)
-        qsh[at, :] = jnp.where(lane2 < 72, qx[at, :].astype(F32), 0.0).astype(BF16)
+        qt[:, at] = qx[at, :].astype(F32).T[0:80].astype(BF16)
         return carry
 
-    lax.fori_loop(0, 8, prepare_keys, 0)
-    wait_all(recv_sems.at[4], do_rcv)
-
-    def prepare_back(i, carry):
-        at = pl.ds(pl.multiple_of(i * 256, 256), 256)
+    lax.fori_loop(0, 8, prepare_queries, 0)
+
+    def attend_back(group_, first):
+        at = pl.ds(group_ * 512, 512)
+        lane5 = lanes((512, 128))
         g = do_rcv[at, :].astype(F32)
         delta = -jnp.sum(g * att_snd[at, :].astype(F32), axis=-1, keepdims=True)
         hi = delta.astype(BF16).astype(F32)
         lo = delta - hi
-        dox[at, :] = jnp.where(lane2 == 72, hi, jnp.where(lane2 == 73, lo, g)).astype(BF16)
-        g = roll(g, 72)
-        dosh[at, 0:128] = jnp.where(lane2 >= 72, g, 0.0).astype(BF16)
-        dosh[at, 128:256] = jnp.where(lane2 < 16, g, 0.0).astype(BF16)
-        return carry
-
-    lax.fori_loop(0, 8, prepare_back, 0)
-    dqt[...] = jnp.zeros_like(dqt)
-
-    def attend_back(i, carry):
-        update = None
-        for s in range(2):
-            at = pl.ds(pl.multiple_of(i * 512 + s * 256, 256), 256)
-            p = pt[at, :]
-            ds = (p.astype(F32) * dot_nt(vx[at, :], dox[...])).astype(BF16)
-            part = dot(kt[:, at], ds)
-            update = part if update is None else update + part
-            dv = dot(p, dosh[...])
-            dk = dot(ds, qsh[...]) * LN2
-            low = (dv[:, 0:128] + dk).astype(BF16)
-            for m in range(4):
-                tail = dv[64 * m : 64 * m + 8, 128:256]
-                for e in range(1, 8):
-                    tail = tail + roll(dv[64 * m + 8 * e : 64 * m + 8 * e + 8, 128:256], 16 * e)
-                slot = i * 8 + s * 4 + m
-                dkv_snd[slot, 0:64] = low[64 * m : 64 * m + 64]
-                dkv_snd[slot, 64:80] = jnp.concatenate([tail, jnp.zeros_like(tail)], axis=0).astype(BF16)
-        dqt[...] += update
-
-        for ii in range(4):
-
-            @pl.when(i == ii)
-            def _():
-                for n in range(8 * ii, 8 * ii + 8):
-                    there = behind(SLOTS[n])
-                    if any(SLOTS[n]):
-                        remote(dkv_snd.at[n], dkv_rcv.at[j], 6, there)
-                    else:
-                        local(dkv_snd.at[n], dkv_rcv.at[j], recv_sems.at[6])
-
-        return carry
-
-    lax.fori_loop(0, 4, attend_back, 0)
-
-    def finish_back(i, carry):
-        at = pl.ds(pl.multiple_of(i * 512, 512), 512)
-        dq_snd[at, :] = (dqt[:, at].T * SCALE).astype(BF16)
-        for ii in range(4):
-
-            @pl.when(i == ii)
-            def _():
-                for n in range(8 * ii, 8 * ii + 8):
-                    there = behind(SLOTS[n])
-                    src = dq_snd.at[pl.ds(64 * n, 64)]
-                    if any(SLOTS[n]):
-                        remote(src, dq_rcv.at[j], 13, there)
-                    else:
-                        local(src, dq_rcv.at[j], recv_sems.at[13])
-
-        return carry
-
-    lax.fori_loop(0, 4, finish_back, 0)
+        dox = jnp.where(lane5 == 72, hi, jnp.where(lane5 == 73, lo, g)).astype(BF16)
+        p = pq[at, :]
+        dv = dot(g.T[0:80].astype(BF16), p)
+        ds = (p.astype(F32) * dot_nt(dox, vx[...])).astype(BF16)
+        dq = dot(ds, kx[...]) * SCALE
+        dq_snd[at, :] = jnp.where(lane5 < 72, dq, 0.0).astype(BF16)
+        dk = dot(qt[:, at], ds)
+        if first:
+            dkt[...] = dk
+            dvt[...] = dv
+        else:
+            dkt[...] += dk
+            dvt[...] += dv
+        for n in range(8 * group_, 8 * group_ + 8):
+            src = dq_snd.at[pl.ds(64 * n, 64)]
+            if any(SLOTS[n]):
+                remote(src, dq_rcv.at[j], 13, behind(SLOTS[n]))
+            else:
+                local(src, dq_rcv.at[j], recv_sems.at[13])
+
+    for group_ in range(4):
+        wait_all(do_sems.at[group_], do_rcv.at[pl.ds(512 * group_, 512)])
+        attend_back(group_, group_ == 0)
+
+    for group_ in range(4):
+        at = slice(group_ * 512, group_ * 512 + 512)
+        low = jnp.concatenate([dkt[0:72, at] * LN2, dvt[0:56, at]], axis=0).T.astype(BF16)
+        for m in range(8):
+            n = 8 * group_ + m
+            dkv_snd[n, 0:64] = low[64 * m : 64 * m + 64]
+            tail = dvt[56:72, 128 * (n // 2) : 128 * (n // 2) + 128]
+            dkv_snd[n, 64:80] = roll(tail, 64 * (n % 2)).astype(BF16)
+            if any(SLOTS[n]):
+                remote(dkv_snd.at[n], dkv_rcv.at[j], 6, behind(SLOTS[n]))
+            else:
+                local(dkv_snd.at[n], dkv_rcv.at[j], recv_sems.at[6])
+
     reduce_second(r1_rcv, r1_z, owns1, 7)
+
+    wait_all(recv_sems.at[13], dq_rcv)
+
+    def both(buffer, h):
+        return jnp.concatenate([buffer[h, 0:64], buffer[HEADS + h, 0:64]], axis=0).astype(F32)
+
+    tiles = [None] * GROUPS
+    for h in range(HEADS):
+        place(tiles, h, roll(both(dq_rcv, h), (HEAD_DIM * h) % 128))
+    for t in range(GROUPS):
+        dproj_b[:, t * 128 : (t + 1) * 128] = tiles[t].astype(BF16)
+    for c in range(3):
+        at = slice(c * 384, (c + 1) * 384)
+        hidp[:, at] = dot_nt(dproj_b[:, 0:D], wsp[at, 0:D])
+    reduce_third(r1_z, r1_chunk, r1_out, chunk1, owns1, 7)
     wait_all(recv_sems.at[6], dkv_rcv)
 
-    def both(buffer, h, part):
-        return jnp.concatenate([buffer[h, part], buffer[HEADS + h, part]], axis=0).astype(F32)
-
+    tails = []
+    for eight in range(2):
+        stack = []
+        for h in range(8 * eight, 8 * eight + 8):
+            first = dkv_rcv[h, 64:80].astype(F32)
+            second = dkv_rcv[HEADS + h, 64:80].astype(F32)
+            stack.append(jnp.where(lanes((16, 128)) < 64, first, roll(second, 64)))
+        tails.append(jnp.concatenate(stack, axis=0).T)
     tiles_k, tiles_v = [None] * GROUPS, [None] * GROUPS
     for h in range(HEADS):
         off = (HEAD_DIM * h) % 128
-        low = both(dkv_rcv, h, slice(0, 64))
-        tails = []
-        for f in range(2):
-            tail = dkv_rcv[f * HEADS + h, 64:80].astype(F32)[0:8]
-            tails += [roll(tail, -16 * e) for e in range(8)]
-        tail = jnp.concatenate(tails, axis=0)
+        low = both(dkv_rcv, h)
+        tail = roll(tails[h // 8], -16 * (h % 8))
         place(tiles_k, h, roll(jnp.where(lane < 72, low, 0.0), off))
         v = jnp.where(lane >= 72, low, jnp.where(lane < 16, tail, 0.0))
         place(tiles_v, h, roll(v, off - 72))
     for t in range(GROUPS):
         dproj_b[:, D + t * 128 : D + (t + 1) * 128] = tiles_k[t].astype(BF16)
         dproj_b[:, 2 * D + t * 128 : 2 * D + (t + 1) * 128] = tiles_v[t].astype(BF16)
-    hidp[...] = jnp.zeros_like(hidp)
-
-    def back1(c, carry):
-        at = pl.ds(pl.multiple_of(c * D, 128), D)
-        hidp[...] += dot_nt(dproj_b[:, at], wsp[:, at])
-        return carry
-
-    lax.fori_loop(1, 3, back1, 0)
-    reduce_third(r1_z, r1_chunk, r1_out, chunk1, owns1, 7)
-    wait_all(recv_sems.at[13], dq_rcv)
-    tiles = [None] * GROUPS
-    for h in range(HEADS):
-        low = jnp.where(lane < 72, both(dq_rcv, h, slice(0, 64)), 0.0)
-        place(tiles, h, roll(low, (HEAD_DIM * h) % 128))
-    for t in range(GROUPS):
-        dproj_b[:, t * 128 : (t + 1) * 128] = tiles[t].astype(BF16)
-    lax.fori_loop(0, 1, back1, 0)
+
+    for c in range(3):
+        at = slice(c * 384, (c + 1) * 384)
+        hidp[:, at] += dot_nt(dproj_b[:, D:], wsp[at, D:])
     adj_rot1 = hidp[...].astype(BF16)
     packed = rotation_gradient(normed1[...].astype(BF16), adj_rot1)
-    for g in range(GROUPS):
-        for s in range(2):
-            r2_snd[2 * g + s] = packed[g][16 * s : 16 * (s + 1)].astype(BF16)
-    reduce_first(r2_snd, r2_rcv, chunk2, owns2, 10)
+    flat = jnp.concatenate(packed, axis=0).astype(BF16)
+    for o in range(6):
+        r2_snd[o] = flat[48 * o : 48 * o + 48]
+    owner = 2 * px + pc
+    owns2 = owner < 6
+    row = [s for s in SLOTS if s[1] == 0]
+    sheet = [s for s in SPACE if s[0] == 0 and s[2] == 0]
+    for step in row:
+        zz, jj = ahead(step)
+        there = 2 * (jj >> 3) + (jj & 1)
+
+        @pl.when(there < 6)
+        def _():
+            if any(step):
+                remote(r2_snd.at[there], r2_rcv.at[owner], 10, (zz, jj))
+            else:
+                local(r2_snd.at[there], r2_rcv.at[owner], recv_sems.at[10])
+
     adj_normed = rotate_transposed(adj_rot1, bd.at[0])
     wait_all(recv_sems.at[5], ah_rcv)
     grad = ah_rcv[...].reshape(TOKENS, D).astype(F32) + normalize_backward(
@@ -651,7 +634,14 @@
     vg[...] = grad.astype(BF16).reshape(2, 64, D)
     vg_out = pltpu.make_async_copy(vg, vg_ref, out_sems.at[0])
     vg_out.start()
-    reduce_second(r2_rcv, r2_z, owns2, 10)
+    @pl.when(owns2)
+    def _():
+        wait_all(recv_sems.at[10], r2_rcv)
+        own = 4 * z + py
+        r2_z[own] = jnp.sum(r2_rcv[...].astype(F32), axis=0).astype(BF16)
+        for step in sheet:
+            remote(r2_z.at[own], r2_z.at[own], 11, ahead(step))
+
     wait_all(send_sems.at[0], vid_mid.at[pl.ds(0, 6)])
     wait_all(send_sems.at[1], ct_mid.at[pl.ds(0, 6)])
     wait_all(send_sems.at[2], qkv_snd.at[pl.ds(0, PWAYS - 1)])
@@ -663,19 +653,37 @@
     wait_all(recv_sems.at[9], r1_out)
     red1 = pltpu.make_async_copy(r1_out, red_ref.at[pl.ds(0, 3 * ROWS)], out_sems.at[1])
     red1.start()
-    reduce_third(r2_z, r2_chunk, r2_out, chunk2, owns2, 10)
+    @pl.when(owns2)
+    def _():
+        wait_all(recv_sems.at[11], r2_z.at[pl.ds(0, 15)])
+        r2_chunk[...] = (jnp.sum(r2_z[...].astype(F32), axis=0) / 128.0).astype(BF16)
+        dst = red_ref.at[pl.ds(pl.multiple_of(3 * ROWS + 48 * owner, 16), 48)]
+        for step in row:
+            if any(step):
+                remote(r2_chunk, dst, 12, ahead(step))
+            else:
+                local(r2_chunk, dst, recv_sems.at[12])
+
     reduce_sent(r1_snd, r1_rcv, r1_z, 27, owns1, 7)
-    reduce_sent(r2_snd, r2_rcv, r2_z, 18, owns2, 10)
-    wait_all(recv_sems.at[12], r2_out)
-    red2 = pltpu.make_async_copy(r2_out, red_ref.at[pl.ds(3 * ROWS, ROWS)], out_sems.at[2])
-    red2.start()
+    @pl.when(owns2)
+    def _():
+        wait_all(send_sems.at[10], r2_snd.at[pl.ds(0, 5)])
+        wait_all(send_sems.at[11], r2_z.at[pl.ds(0, 15)])
+        wait_all(send_sems.at[12], r2_rcv.at[pl.ds(0, 7)])
+
+    @pl.when(jnp.logical_not(owns2))
+    def _():
+        wait_all(send_sems.at[10], r2_snd)
+
+    wait_all(recv_sems.at[12], red_ref.at[pl.ds(3 * ROWS, ROWS)])
     red1.wait()
     vg_out.wait()
-    red2.wait()
-
-
-def unpack_kernel(red, vg_in, vg_out, sout, tin, tout, sin, sem):
-    copy = pltpu.make_async_copy(vg_in, vg_out, sem)
+
+
+def unpack_kernel(red_h, vg_in, vg_out, sout, tin, tout, sin, red, vg, terms, sems):
+    load = pltpu.make_async_copy(red_h, red, sems.at[0])
+    load.start()
+    copy = pltpu.make_async_copy(vg_in, vg, sems.at[1])
     copy.start()
     shape = (BLOCK, 40, ROWS)
     b = lax.broadcasted_iota(jnp.int32, shape, 0)
@@ -687,6 +695,10 @@
     own = ((n & 3) == (lax.broadcasted_iota(jnp.int32, shape, 2) >> 5)).reshape(BLOCK * 40, 128)
     repeat = jnp.where(lanes((128, 128)) % BLOCK == rows((128, 128)) % BLOCK, 1.0, 0.0).astype(BF16)
     lane = lanes((40, 128)) >> 5
+    copy.wait()
+    stores = [pltpu.make_async_copy(vg, vg_out, sems.at[1])]
+    stores[0].start()
+    load.wait()
     for term, out in enumerate((sout, tin, tout, sin)):
         wide = dot(pick, red[term * ROWS : (term + 1) * ROWS, :])
         wide = dot(jnp.where(own, wide, 0.0).astype(BF16), repeat)
@@ -695,8 +707,11 @@
             for s in range(4):
                 at = (4 * m + s) * 40
                 four = jnp.where(lane == s, wide[at : at + 40], four)
-            out[4 * m : 4 * m + 4] = four.T[:, 0:NBLOCK].reshape(4, BLOCK, NBLOCK)
-    copy.wait()
+            terms[term, 4 * m : 4 * m + 4] = four.T[:, 0:NBLOCK].reshape(4, BLOCK, NBLOCK)
+        stores.append(pltpu.make_async_copy(terms.at[term], out, sems.at[2 + term]))
+        stores[-1].start()
+    for store in stores:
+        store.wait()
 
 
 def per_device(
@@ -729,18 +744,16 @@
         vm((HEADS, TOKENS, TOKENS), BF16), vm((HEADS, TOKENS, TOKENS), BF16),
         vm((FRAMES, 16, D), BF16), vm((2, 64, D), BF16),
         vm((FRAMES, HEADS, 16, 128), BF16), vm((PATCHES, 128), BF16),
-        vm((PATCHES, 128), BF16), vm((PATCHES, 256), BF16), vm((PATCHES, 128), BF16),
-        vm((128, PATCHES), BF16), vm((128, PATCHES), F32), vm((PATCHES, PATCHES), BF16),
+        vm((80, PATCHES), BF16), vm((80, PATCHES), F32), vm((80, PATCHES), F32), vm((PATCHES, PATCHES), BF16),
         vm((PWAYS, 80, 128), BF16), vm((PWAYS, 80, 128), BF16),
         vm((PATCHES, 128), BF16), vm((PWAYS, 64, 128), BF16), vm((2, 64, D), BF16),
         vm((27, 32, 128), BF16), vm((PWAYS, 32, 128), BF16), vm((ZWAYS, 32, 128), F32),
         vm((32, 128), BF16), vm((3 * ROWS, 128), BF16),
-        vm((18, 16, 128), BF16), vm((PWAYS, 16, 128), BF16), vm((ZWAYS, 16, 128), F32),
-        vm((16, 128), BF16), vm((ROWS, 128), BF16),
-        dma((10,)), dma((3,)), dma((14,)), dma((14,)), dma((4,)),
+        vm((6, 48, 128), BF16), vm((8, 48, 128), BF16), vm((16, 48, 128), BF16),
+        vm((48, 128), BF16),
+        dma((12,)), dma((3,)), dma((14,)), dma((14,)), dma((4,)), dma((4,)),
     ]
     anyspec = pl.BlockSpec(memory_space=pl.ANY)
-    vspec = pl.BlockSpec(memory_space=pltpu.VMEM)
     blocks = [r.transpose(1, 2, 0) for r in (spatial_inward, spatial_outward, temporal_inward, temporal_outward)]
     grad, red = pl.pallas_call(
         kernel,
@@ -763,10 +776,12 @@
     grad, sout, tin, tout, sin = pl.pallas_call(
         unpack_kernel,
         out_shape=(jax.ShapeDtypeStruct((2, 64, D), BF16), term, term, term, term),
-        in_specs=[vspec, anyspec],
-        out_specs=(anyspec, vspec, vspec, vspec, vspec),
-        scratch_shapes=[dma],
-        compiler_params=pltpu.CompilerParams(vmem_limit_bytes=32 * 1024 * 1024),
+        in_specs=[anyspec] * 2,
+        out_specs=(anyspec,) * 5,
+        scratch_shapes=[
+            vm((4 * ROWS, 128), BF16), vm((2, 64, D), BF16), vm((4, BLOCK, BLOCK, NBLOCK), F32), dma((6,)),
+        ],
+        compiler_params=pltpu.CompilerParams(vmem_limit_bytes=62 * 1024 * 1024),
         name="unpack_terms",
     )(red, grad)
     sin, sout, tin, tout = (r.transpose(2, 0, 1) for r in (sin, sout, tin, tout))

time: 102 us -> 93.6 us (0.918)
  Pallas kernels: 99.1 us -> 92.6 us
  local copies, waits for them, and re-layouts: 1.92 us -> 0 us
    pallas_call x1, Pallas kernels: 95.9 us -> 88.8 us  [per_device(): pl.pallas_call(kernel, out_shape=(jax.ShapeDtypeStruct((2, 64, D), BF16),...]
    unnamed x4 -> x0, local copies, waits for them, and re-layouts: 1.92 us -> none
where the time goes in v2:
time: 93.6 us; the launch traced here: 93.5 us
  Pallas kernels  92.6 us (99%)
    pallas_call x1, Pallas kernels, per_device(): pl.pallas_call(kernel, out_shape=(jax.ShapeDtypeStruct((2, 64, D), BF16),...  88.8 us
    pallas_call x1, Pallas kernels, per_device(): pl.pallas_call(unpack_kernel, out_shape=(jax.ShapeDtypeStruct((2, 64, D),...  3.87 us

profile of v2, /device:TPU:1, one launch (start us, length us, event | category | flops | bytes accessed | tf_op | source)
XLA Modules:
  0.0 93.5 jit_solution(14149463215002585435)
XLA Ops:
  0.6 88.8 %block_backward.1 = (bf16[2,64,1152]{2,1,0:T(8,128)(2,1)}, bf16[1152,128]{1,0:T(8,128)(2,1)}) custom-call(s32[8]{0:T(128)} %mask_ref.1, bf16[2,64,1152]{2,1,0:T(8,128)(2,1)} %video.1, bf16[2,64,1152]{2,1,0:T(8,128)(2,1)} %cotangent.1, bf16[1152,3456]{1,0:T(8,128)(2,1)} %wsp_h.1, bf16[1152,1152]{1,0:T(8,128)(2,1)} %wso_h.1, bf16[1152,3456]{1,0:T(8,128)(2,1)} %wtp_h.1, ...), custom_call_target="tpu_custom_call" | custom-call | tf_op jit(solution)/shard_map/block_backward/pallas_call | solution.py:758
  89.4 3.9 %unpack_terms.1 = (bf16[2,64,1152]{2,1,0:T(8,128)(2,1)}, f32[32,32,36]{2,1,0:T(8,128)}, f32[32,32,36]{2,1,0:T(8,128)}, f32[32,32,36]{2,1,0:T(8,128)}, f32[32,32,36]{2,1,0:T(8,128)}) custom-call(bf16[1152,128]{1,0:T(8,128)(2,1)} %get-tuple-element.12.red_h, bf16[2,64,1152]{2,1,0:T(8,128)(2,1)} %get-tuple-element.13.vg_in), custom_call_target="tpu_custom_call" | custom-call | tf_op jit(solution)/shard_map/unpack_terms/pallas_call | solution.py:776

commit v3 on v2

--- a/solution.py
+++ b/solution.py
@@ -114,9 +114,35 @@
     return packed
 
 
+def layout_tools():
+    shape = (BLOCK, 40, ROWS)
+    b = lax.broadcasted_iota(jnp.int32, shape, 0)
+    n = lax.broadcasted_iota(jnp.int32, shape, 1)
+    from_row = lax.broadcasted_iota(jnp.int32, shape, 2)
+    pick = jnp.where(from_row == (n >> 2) * BLOCK + b, 1.0, 0.0).reshape(BLOCK * 40, ROWS).astype(BF16)
+    shape = (BLOCK, 40, 128)
+    n = lax.broadcasted_iota(jnp.int32, shape, 1)
+    own = ((n & 3) == (lax.broadcasted_iota(jnp.int32, shape, 2) >> 5)).reshape(BLOCK * 40, 128)
+    repeat = jnp.where(lanes((128, 128)) % BLOCK == rows((128, 128)) % BLOCK, 1.0, 0.0).astype(BF16)
+    return pick, own, repeat
+
+
+def lay_out(tools, term, out):
+    pick, own, repeat = tools
+    lane = lanes((40, 128)) >> 5
+    wide = dot(pick, term)
+    wide = dot(jnp.where(own, wide, 0.0).astype(BF16), repeat)
+    for m in range(8):
+        four = jnp.zeros((40, 128), F32)
+        for s in range(4):
+            at = (4 * m + s) * 40
+            four = jnp.where(lane == s, wide[at : at + 40], four)
+        out[4 * m : 4 * m + 4] = four.T[:, 0:NBLOCK].reshape(4, BLOCK, NBLOCK)
+
+
 def kernel(
     mask_ref, video, cotangent, wsp_h, wso_h, wtp_h, wto_h, rsi_h, rso_h, rti_h, rto_h,
-    vg_ref, red_ref,
+    vg_ref, terms_ref, red_ref,
     wsp, wso, wtp, wto, r4, bd32, bd,
     vid, cot, vid_mid, ct_mid,
     normed1, inverse1, rot_b, proj,
@@ -125,9 +151,9 @@
     hidp, normed2, proj2, att2_b, dproj_b,
     t_s, t_dp, t_p, t_ds,
     ah_snd, ah_rcv, do_snd, do_rcv, qt, dkt, dvt, pq,
-    dkv_snd, dkv_rcv, dq_snd, dq_rcv, vg,
+    dk_snd, dk_rcv, dv_snd, dv_rcv, dq_snd, dq_rcv, dq_last, w_last, vg, dpt, adjt,
     r1_snd, r1_rcv, r1_z, r1_chunk, r1_out,
-    r2_snd, r2_rcv, r2_z, r2_chunk,
+    r2_snd, r2_rcv, r2_z, r2_chunk, terms,
     load_sems, out_sems, send_sems, recv_sems, qkv_sems, do_sems,
 ):
     z = lax.axis_index("frame")
@@ -195,12 +221,10 @@
         bd[index] = bd32[...].astype(BF16)
 
     early[0].wait()
-    normed, inverse = normalize(vid[...].reshape(TOKENS, D).astype(F32))
-    normed1[...] = normed
-    inverse1[...] = inverse
+    normed, _ = normalize(vid[...].reshape(TOKENS, D).astype(F32))
     early[1].wait()
     make_blocks(0)
-    rot_b[...] = rotate(normed1[...].astype(BF16), bd.at[0]).astype(BF16)
+    rot_b[...] = rotate(normed.astype(BF16), bd.at[0]).astype(BF16)
 
     for c in range(3):
         at = slice(c * D, (c + 1) * D)
@@ -251,6 +275,18 @@
     for n in (1, 2, 3):
         late[n].wait()
         make_blocks(n)
+
+    columns = vid[...].reshape(TOKENS, D).astype(F32).T
+    columns = columns - jnp.mean(columns, axis=0, keepdims=True)
+    inverse = lax.rsqrt(jnp.mean(columns * columns, axis=0, keepdims=True) + EPSILON)
+    normed1[...] = columns * inverse
+    inverse1[...] = jnp.broadcast_to(inverse, (8, 128))
+
+    shape = (D, 128)
+    column = HEAD_DIM * (lanes(shape) >> 3) + 64 + (lanes(shape) & 7)
+    select = jnp.where(rows(shape) == column, 1.0, 0.0).astype(BF16)
+    for n, section in enumerate((0, 2)):
+        w_last[n] = dot(wsp[:, section * D : (section + 1) * D], select).astype(BF16)
 
     wait_all(recv_sems.at[1], ct_mid)
     frame_row = rows((TOKENS, 1)) // 16
@@ -427,7 +463,7 @@
         piece = jnp.where(lane < 72, roll(first, -off), 0.0).astype(BF16)
         do_snd[:, h] = piece.reshape(FRAMES, 16, 128)
 
-    for step in SPACE + [(0, 0, 0, 0)]:
+    for step in [slot[:3] + (d,) for slot in SLOTS for d in (2, 1, 3, 0)]:
         zz, jj = ahead(step)
         src = do_snd.at[2 * zz + (jj >> 4), jj & 15]
         n = SLOT_OF[step[:3]]
@@ -521,7 +557,19 @@
 
     lax.fori_loop(0, 8, prepare_queries, 0)
 
-    def attend_back(group_, first):
+    def beside(left, right, odd):
+        left, right = (roll(left, 64), right) if odd else (left, roll(right, 64))
+        return jnp.where(lanes(left.shape) < 64, left, right)
+
+    def value_gradient(group_):
+        at = pl.ds(group_ * 512, 512)
+        dv = dot(do_rcv[at, :].astype(F32).T[0:80].astype(BF16), pq[at, :])
+        if group_ == 0:
+            dvt[...] = dv
+        else:
+            dvt[...] += dv
+
+    def attend_back(group_):
         at = pl.ds(group_ * 512, 512)
         lane5 = lanes((512, 128))
         g = do_rcv[at, :].astype(F32)
@@ -529,85 +577,95 @@
         hi = delta.astype(BF16).astype(F32)
         lo = delta - hi
         dox = jnp.where(lane5 == 72, hi, jnp.where(lane5 == 73, lo, g)).astype(BF16)
-        p = pq[at, :]
-        dv = dot(g.T[0:80].astype(BF16), p)
-        ds = (p.astype(F32) * dot_nt(dox, vx[...])).astype(BF16)
-        dq = dot(ds, kx[...]) * SCALE
-        dq_snd[at, :] = jnp.where(lane5 < 72, dq, 0.0).astype(BF16)
+        ds = (pq[at, :].astype(F32) * dot_nt(dox, vx[...])).astype(BF16)
+        dq = dot(ds, kx[...]).T * SCALE
+        for m in range(8):
+            tile = dq[:, 128 * (m // 2) : 128 * (m // 2) + 128]
+            dq_snd[8 * group_ + m] = beside(tile[0:32], tile[32:64], m % 2).astype(BF16)
+        dq_last[:, group_ * 512 : group_ * 512 + 512] = dq[64:72]
         dk = dot(qt[:, at], ds)
-        if first:
+        if group_ == 0:
             dkt[...] = dk
-            dvt[...] = dv
         else:
             dkt[...] += dk
-            dvt[...] += dv
-        for n in range(8 * group_, 8 * group_ + 8):
-            src = dq_snd.at[pl.ds(64 * n, 64)]
+        send_back(dq_snd, dq_rcv, 13, range(8 * group_, 8 * group_ + 8))
+
+    def send_back(snd, rcv, phase, slots):
+        for n in slots:
             if any(SLOTS[n]):
-                remote(src, dq_rcv.at[j], 13, behind(SLOTS[n]))
+                remote(snd.at[n], rcv.at[j], phase, behind(SLOTS[n]))
             else:
-                local(src, dq_rcv.at[j], recv_sems.at[13])
+                local(snd.at[n], rcv.at[j], recv_sems.at[phase])
 
     for group_ in range(4):
         wait_all(do_sems.at[group_], do_rcv.at[pl.ds(512 * group_, 512)])
-        attend_back(group_, group_ == 0)
-
-    for group_ in range(4):
-        at = slice(group_ * 512, group_ * 512 + 512)
-        low = jnp.concatenate([dkt[0:72, at] * LN2, dvt[0:56, at]], axis=0).T.astype(BF16)
-        for m in range(8):
-            n = 8 * group_ + m
-            dkv_snd[n, 0:64] = low[64 * m : 64 * m + 64]
-            tail = dvt[56:72, 128 * (n // 2) : 128 * (n // 2) + 128]
-            dkv_snd[n, 64:80] = roll(tail, 64 * (n % 2)).astype(BF16)
-            if any(SLOTS[n]):
-                remote(dkv_snd.at[n], dkv_rcv.at[j], 6, behind(SLOTS[n]))
-            else:
-                local(dkv_snd.at[n], dkv_rcv.at[j], recv_sems.at[6])
+        value_gradient(group_)
+        if group_ == 0:
+            attend_back(0)
+    for n in range(PWAYS):
+        at = slice(128 * (n // 2), 128 * (n // 2) + 128)
+        dv_snd[n] = beside(dvt[0:32, at], dvt[32:64, at], n % 2).astype(BF16)
+    send_back(dv_snd, dv_rcv, 15, range(PWAYS))
+    for group_ in (1, 2, 3):
+        attend_back(group_)
+
+    for n in range(PWAYS):
+        at = slice(128 * (n // 2), 128 * (n // 2) + 128)
+        rest = [dkt[48:72, at] * LN2, dq_last[:, at], dvt[64:72, at], jnp.zeros((8, 128), F32)]
+        dk_snd[n] = beside(dkt[0:48, at] * LN2, jnp.concatenate(rest, axis=0), n % 2).astype(BF16)
+    send_back(dk_snd, dk_rcv, 6, range(PWAYS))
 
     reduce_second(r1_rcv, r1_z, owns1, 7)
 
-    wait_all(recv_sems.at[13], dq_rcv)
-
-    def both(buffer, h):
-        return jnp.concatenate([buffer[h, 0:64], buffer[HEADS + h, 0:64]], axis=0).astype(F32)
-
-    tiles = [None] * GROUPS
-    for h in range(HEADS):
-        place(tiles, h, roll(both(dq_rcv, h), (HEAD_DIM * h) % 128))
-    for t in range(GROUPS):
-        dproj_b[:, t * 128 : (t + 1) * 128] = tiles[t].astype(BF16)
+    def halves(buffer, h):
+        one, two = buffer[h].astype(F32), buffer[HEADS + h].astype(F32)
+        first = lanes(one.shape) < 64
+        return jnp.where(first, one, roll(two, 64)), jnp.where(first, roll(one, 64), two)
+
+    def unpack_first(buffer, base):
+        for pair in range(HEADS // 2):
+            parts = []
+            for h in (2 * pair, 2 * pair + 1):
+                parts += [*halves(buffer, h), jnp.zeros((8, 128), F32)]
+            at = base + 144 * pair
+            dpt[at : at + 144] = jnp.concatenate(parts, axis=0).astype(BF16)
+
+    wait_all(recv_sems.at[15], dv_rcv)
+    unpack_first(dv_rcv, 2 * D)
     for c in range(3):
         at = slice(c * 384, (c + 1) * 384)
-        hidp[:, at] = dot_nt(dproj_b[:, 0:D], wsp[at, 0:D])
-    reduce_third(r1_z, r1_chunk, r1_out, chunk1, owns1, 7)
-    wait_all(recv_sems.at[6], dkv_rcv)
-
-    tails = []
-    for eight in range(2):
-        stack = []
-        for h in range(8 * eight, 8 * eight + 8):
-            first = dkv_rcv[h, 64:80].astype(F32)
-            second = dkv_rcv[HEADS + h, 64:80].astype(F32)
-            stack.append(jnp.where(lanes((16, 128)) < 64, first, roll(second, 64)))
-        tails.append(jnp.concatenate(stack, axis=0).T)
-    tiles_k, tiles_v = [None] * GROUPS, [None] * GROUPS
-    for h in range(HEADS):
-        off = (HEAD_DIM * h) % 128
-        low = both(dkv_rcv, h)
-        tail = roll(tails[h // 8], -16 * (h % 8))
-        place(tiles_k, h, roll(jnp.where(lane < 72, low, 0.0), off))
-        v = jnp.where(lane >= 72, low, jnp.where(lane < 16, tail, 0.0))
-        place(tiles_v, h, roll(v, off - 72))
-    for t in range(GROUPS):
-        dproj_b[:, D + t * 128 : D + (t + 1) * 128] = tiles_k[t].astype(BF16)
-        dproj_b[:, 2 * D + t * 128 : 2 * D + (t + 1) * 128] = tiles_v[t].astype(BF16)
-
+        adjt[at] = dot(wsp[at, 2 * D :], dpt[2 * D :])
+    wait_all(recv_sems.at[13], dq_rcv)
+    unpack_first(dq_rcv, 0)
     for c in range(3):
         at = slice(c * 384, (c + 1) * 384)
-        hidp[:, at] += dot_nt(dproj_b[:, D:], wsp[at, D:])
-    adj_rot1 = hidp[...].astype(BF16)
-    packed = rotation_gradient(normed1[...].astype(BF16), adj_rot1)
+        adjt[at] += dot(wsp[at, 0:D], dpt[0:D])
+    reduce_third(r1_z, r1_chunk, r1_out, chunk1, owns1, 7)
+    wait_all(recv_sems.at[6], dk_rcv)
+
+    last = [[], []]
+    for pair in range(HEADS // 2):
+        parts = []
+        for h in (2 * pair, 2 * pair + 1):
+            left, right = halves(dk_rcv, h)
+            parts += [left, right[0:24]]
+            last[0].append(right[24:32])
+            last[1].append(right[32:40])
+        at = D + 144 * pair
+        dpt[at : at + 144] = jnp.concatenate(parts, axis=0).astype(BF16)
+    last = [jnp.concatenate(parts, axis=0).astype(BF16) for parts in last]
+
+    for c in range(3):
+        at = slice(c * 384, (c + 1) * 384)
+        adjt[at] += (
+            dot(wsp[at, D : 2 * D], dpt[D : 2 * D]) + dot(w_last[0, at], last[0]) + dot(w_last[1, at], last[1])
+        )
+    packed = []
+    mask = block_mask((128, 128))
+    for g in range(GROUPS):
+        at = slice(g * 128, (g + 1) * 128)
+        full = jnp.where(mask, dot_nt(normed1[at].astype(BF16), adjt[at].astype(BF16)), 0.0)
+        packed.append(full[0:32] + full[32:64] + full[64:96] + full[96:128])
     flat = jnp.concatenate(packed, axis=0).astype(BF16)
     for o in range(6):
         r2_snd[o] = flat[48 * o : 48 * o + 48]
@@ -626,11 +684,18 @@
             else:
                 local(r2_snd.at[there], r2_rcv.at[owner], recv_sems.at[10])
 
-    adj_normed = rotate_transposed(adj_rot1, bd.at[0])
+    adj_normed = jnp.concatenate(
+        [
+            dot(bd[0, g * 128 : (g + 1) * 128, :], adjt[g * 128 : (g + 1) * 128].astype(BF16))
+            for g in range(GROUPS)
+        ],
+        axis=0,
+    )
+    grad_mean = jnp.mean(adj_normed, axis=0, keepdims=True)
+    grad_cross = jnp.mean(adj_normed * normed1[...], axis=0, keepdims=True)
+    grad = (inverse1[0:1] * (adj_normed - grad_mean - normed1[...] * grad_cross)).T
     wait_all(recv_sems.at[5], ah_rcv)
-    grad = ah_rcv[...].reshape(TOKENS, D).astype(F32) + normalize_backward(
-        adj_normed, normed1[...], inverse1[...]
-    )
+    grad = ah_rcv[...].reshape(TOKENS, D).astype(F32) + grad
     vg[...] = grad.astype(BF16).reshape(2, 64, D)
     vg_out = pltpu.make_async_copy(vg, vg_ref, out_sems.at[0])
     vg_out.start()
@@ -648,22 +713,26 @@
     wait_all(send_sems.at[3], att_snd.at[pl.ds(0, PATCHES - 16)])
     wait_all(send_sems.at[4], do_rcv.at[pl.ds(0, PATCHES - 16)])
     wait_all(send_sems.at[5], ah_snd.at[pl.ds(0, 6)])
-    wait_all(send_sems.at[6], dkv_snd.at[pl.ds(0, PWAYS - 1)])
-    wait_all(send_sems.at[13], dq_snd.at[pl.ds(0, PATCHES - 64)])
+    wait_all(send_sems.at[6], dk_snd.at[pl.ds(0, PWAYS - 1)])
+    wait_all(send_sems.at[15], dv_snd.at[pl.ds(0, PWAYS - 1)])
+    wait_all(send_sems.at[13], dq_snd.at[pl.ds(0, PWAYS - 1)])
     wait_all(recv_sems.at[9], r1_out)
-    red1 = pltpu.make_async_copy(r1_out, red_ref.at[pl.ds(0, 3 * ROWS)], out_sems.at[1])
-    red1.start()
     @pl.when(owns2)
     def _():
         wait_all(recv_sems.at[11], r2_z.at[pl.ds(0, 15)])
         r2_chunk[...] = (jnp.sum(r2_z[...].astype(F32), axis=0) / 128.0).astype(BF16)
-        dst = red_ref.at[pl.ds(pl.multiple_of(3 * ROWS + 48 * owner, 16), 48)]
+        dst = red_ref.at[pl.ds(pl.multiple_of(48 * owner, 16), 48)]
         for step in row:
             if any(step):
                 remote(r2_chunk, dst, 12, ahead(step))
             else:
                 local(r2_chunk, dst, recv_sems.at[12])
 
+    tools = layout_tools()
+    for n in range(3):
+        lay_out(tools, r1_out[n * ROWS : (n + 1) * ROWS], terms.at[n])
+    red1 = pltpu.make_async_copy(terms, terms_ref, out_sems.at[1])
+    red1.start()
     reduce_sent(r1_snd, r1_rcv, r1_z, 27, owns1, 7)
     @pl.when(owns2)
     def _():
@@ -675,41 +744,26 @@
     def _():
         wait_all(send_sems.at[10], r2_snd)
 
-    wait_all(recv_sems.at[12], red_ref.at[pl.ds(3 * ROWS, ROWS)])
+    wait_all(recv_sems.at[12], red_ref)
     red1.wait()
     vg_out.wait()
 
 
-def unpack_kernel(red_h, vg_in, vg_out, sout, tin, tout, sin, red, vg, terms, sems):
-    load = pltpu.make_async_copy(red_h, red, sems.at[0])
-    load.start()
-    copy = pltpu.make_async_copy(vg_in, vg, sems.at[1])
-    copy.start()
-    shape = (BLOCK, 40, ROWS)
-    b = lax.broadcasted_iota(jnp.int32, shape, 0)
-    n = lax.broadcasted_iota(jnp.int32, shape, 1)
-    from_row = lax.broadcasted_iota(jnp.int32, shape, 2)
-    pick = jnp.where(from_row == (n >> 2) * BLOCK + b, 1.0, 0.0).reshape(BLOCK * 40, ROWS).astype(BF16)
-    shape = (BLOCK, 40, 128)
-    n = lax.broadcasted_iota(jnp.int32, shape, 1)
-    own = ((n & 3) == (lax.broadcasted_iota(jnp.int32, shape, 2) >> 5)).reshape(BLOCK * 40, 128)
-    repeat = jnp.where(lanes((128, 128)) % BLOCK == rows((128, 128)) % BLOCK, 1.0, 0.0).astype(BF16)
-    lane = lanes((40, 128)) >> 5
-    copy.wait()
-    stores = [pltpu.make_async_copy(vg, vg_out, sems.at[1])]
-    stores[0].start()
-    load.wait()
-    for term, out in enumerate((sout, tin, tout, sin)):
-        wide = dot(pick, red[term * ROWS : (term + 1) * ROWS, :])
-        wide = dot(jnp.where(own, wide, 0.0).astype(BF16), repeat)
-        for m in range(8):
-            four = jnp.zeros((40, 128), F32)
-            for s in range(4):
-                at = (4 * m + s) * 40
-                four = jnp.where(lane == s, wide[at : at + 40], four)
-            terms[term, 4 * m : 4 * m + 4] = four.T[:, 0:NBLOCK].reshape(4, BLOCK, NBLOCK)
-        stores.append(pltpu.make_async_copy(terms.at[term], out, sems.at[2 + term]))
-        stores[-1].start()
+def unpack_kernel(sin_h, terms_h, vg_in, vg_out, sout, tin, tout, sin, packed, terms, vg, in_sems, out_sems):
+    loads = [pltpu.make_async_copy(sin_h, packed, in_sems.at[0])]
+    loads += [pltpu.make_async_copy(terms_h.at[n], terms.at[n], in_sems.at[n + 1]) for n in range(3)]
+    loads.append(pltpu.make_async_copy(vg_in, vg, in_sems.at[4]))
+    for copy in loads:
+        copy.start()
+    stores = [pltpu.make_async_copy(terms.at[n], out, out_sems.at[n]) for n, out in enumerate((sout, tin, tout, sin))]
+    stores.append(pltpu.make_async_copy(vg, vg_out, out_sems.at[4]))
+    tools = layout_tools()
+    loads[0].wait()
+    lay_out(tools, packed[...], terms.at[3])
+    stores[3].start()
+    for n, at in ((1, 0), (2, 1), (3, 2), (4, 4)):
+        loads[n].wait()
+        stores[at].start()
     for store in stores:
         store.wait()
 
@@ -733,7 +787,7 @@
         vm((D, 3 * D), BF16), vm((D, D), BF16), vm((D, 3 * D), BF16), vm((D, D), BF16),
         vm((4, BLOCK, BLOCK, NBLOCK), F32), vm((D, 128), F32), vm((4, D, 128), BF16),
         vm((2, 64, D), BF16), vm((2, 64, D), BF16), vm((FRAMES, 16, D), BF16), vm((FRAMES, 16, D), BF16),
-        vm((TOKENS, D), F32), vm((TOKENS, 1), F32), vm((TOKENS, D), BF16), vm((TOKENS, 3 * D), F32),
+        vm((D, TOKENS), F32), vm((8, TOKENS), F32), vm((TOKENS, D), BF16), vm((TOKENS, 3 * D), F32),
         vm((PWAYS, 64, 256), BF16), vm((PATCHES, 256), BF16),
         vm((PATCHES, 128), BF16), vm((PATCHES, 128), BF16), vm((PATCHES, 128), BF16),
         vm((PATCHES, 128), BF16), vm((FRAMES, HEADS, 16, 128), BF16), vm((TOKENS, D), BF16),
@@ -745,24 +799,27 @@
         vm((FRAMES, 16, D), BF16), vm((2, 64, D), BF16),
         vm((FRAMES, HEADS, 16, 128), BF16), vm((PATCHES, 128), BF16),
         vm((80, PATCHES), BF16), vm((80, PATCHES), F32), vm((80, PATCHES), F32), vm((PATCHES, PATCHES), BF16),
-        vm((PWAYS, 80, 128), BF16), vm((PWAYS, 80, 128), BF16),
-        vm((PATCHES, 128), BF16), vm((PWAYS, 64, 128), BF16), vm((2, 64, D), BF16),
+        vm((PWAYS, 48, 128), BF16), vm((PWAYS, 48, 128), BF16), vm((PWAYS, 32, 128), BF16), vm((PWAYS, 32, 128), BF16),
+        vm((PWAYS, 32, 128), BF16), vm((PWAYS, 32, 128), BF16), vm((8, PATCHES), F32), vm((2, D, 128), BF16),
+        vm((2, 64, D), BF16),
+        vm((3 * D, TOKENS), BF16), vm((D, TOKENS), F32),
         vm((27, 32, 128), BF16), vm((PWAYS, 32, 128), BF16), vm((ZWAYS, 32, 128), F32),
         vm((32, 128), BF16), vm((3 * ROWS, 128), BF16),
         vm((6, 48, 128), BF16), vm((8, 48, 128), BF16), vm((16, 48, 128), BF16),
-        vm((48, 128), BF16),
-        dma((12,)), dma((3,)), dma((14,)), dma((14,)), dma((4,)), dma((4,)),
+        vm((48, 128), BF16), vm((3, BLOCK, BLOCK, NBLOCK), F32),
+        dma((12,)), dma((3,)), dma((16,)), dma((16,)), dma((4,)), dma((4,)),
     ]
     anyspec = pl.BlockSpec(memory_space=pl.ANY)
     blocks = [r.transpose(1, 2, 0) for r in (spatial_inward, spatial_outward, temporal_inward, temporal_outward)]
-    grad, red = pl.pallas_call(
+    grad, terms, red = pl.pallas_call(
         kernel,
         out_shape=(
             jax.ShapeDtypeStruct((2, 64, D), BF16),
-            jax.ShapeDtypeStruct((4 * ROWS, 128), BF16),
+            jax.ShapeDtypeStruct((3, BLOCK, BLOCK, NBLOCK), F32),
+            jax.ShapeDtypeStruct((ROWS, 128), BF16),
         ),
         in_specs=[pl.BlockSpec(memory_space=pltpu.SMEM)] + [anyspec] * 10,
-        out_specs=(anyspec, anyspec),
+        out_specs=(anyspec,) * 3,
         scratch_shapes=scratch,
         compiler_params=pltpu.CompilerParams(
             collective_id=0, has_side_effects=True, vmem_limit_bytes=62 * 1024 * 1024
@@ -776,14 +833,14 @@
     grad, sout, tin, tout, sin = pl.pallas_call(
         unpack_kernel,
         out_shape=(jax.ShapeDtypeStruct((2, 64, D), BF16), term, term, term, term),
-        in_specs=[anyspec] * 2,
+        in_specs=[anyspec] * 3,
         out_specs=(anyspec,) * 5,
         scratch_shapes=[
-            vm((4 * ROWS, 128), BF16), vm((2, 64, D), BF16), vm((4, BLOCK, BLOCK, NBLOCK), F32), dma((6,)),
+            vm((ROWS, 128), BF16), vm((4, BLOCK, BLOCK, NBLOCK), F32), vm((2, 64, D), BF16), dma((5,)), dma((5,)),
         ],
         compiler_params=pltpu.CompilerParams(vmem_limit_bytes=62 * 1024 * 1024),
         name="unpack_terms",
-    )(red, grad)
+    )(red, terms, grad)
     sin, sout, tin, tout = (r.transpose(2, 0, 1) for r in (sin, sout, tin, tout))
     return grad, sin, sout, tin, tout
 

time: 93.6 us -> 90.7 us (0.969)
  Pallas kernels: 92.6 us -> 89.8 us
    pallas_call x1, Pallas kernels: 88.8 us -> 86.7 us  [per_device(): pl.pallas_call(kernel, out_shape=(jax.ShapeDtypeStruct((2, 64, D), BF16),...]
where the time goes in v3:
time: 90.7 us; the launch traced here: 90.6 us
  Pallas kernels  89.8 us (99%)
    pallas_call x1, Pallas kernels, per_device(): pl.pallas_call(kernel, out_shape=(jax.ShapeDtypeStruct((2, 64, D), BF16),...  86.7 us
    pallas_call x1, Pallas kernels, per_device(): pl.pallas_call(unpack_kernel, out_shape=(jax.ShapeDtypeStruct((2, 64, D),...  3.08 us

profile of v3, /device:TPU:1, one launch (start us, length us, event | category | flops | bytes accessed | tf_op | source)
XLA Modules:
  0.0 90.6 jit_solution(10654437916419365791)
XLA Ops:
  0.6 86.7 %block_backward.1 = (bf16[2,64,1152]{2,1,0:T(8,128)(2,1)}, f32[3,32,32,36]{3,2,1,0:T(8,128)}, bf16[288,128]{1,0:T(8,128)(2,1)}) custom-call(s32[8]{0:T(128)} %mask_ref.1, bf16[2,64,1152]{2,1,0:T(8,128)(2,1)} %video.1, bf16[2,64,1152]{2,1,0:T(8,128)(2,1)} %cotangent.1, bf16[1152,3456]{1,0:T(8,128)(2,1)} %wsp_h.1, bf16[1152,1152]{1,0:T(8,128)(2,1)} %wso_h.1, ...), custom_call_target="tpu_custom_call" | custom-call | tf_op jit(solution)/shard_map/block_backward/pallas_call | solution.py:814
  87.3 3.1 %unpack_terms.1 = (bf16[2,64,1152]{2,1,0:T(8,128)(2,1)}, f32[32,32,36]{2,1,0:T(8,128)}, f32[32,32,36]{2,1,0:T(8,128)}, f32[32,32,36]{2,1,0:T(8,128)}, f32[32,32,36]{2,1,0:T(8,128)}) custom-call(bf16[288,128]{1,0:T(8,128)(2,1)} %get-tuple-element.13.sin_h, f32[3,32,32,36]{3,2,1,0:T(8,128)} %get-tuple-element.14.terms_h, ...), custom_call_target="tpu_custom_call" | custom-call | tf_op jit(solution)/shard_map/unpack_terms/pallas_call | solution.py:833

commit v4 on v3

--- a/solution.py
+++ b/solution.py
@@ -146,11 +146,11 @@
     wsp, wso, wtp, wto, r4, bd32, bd,
     vid, cot, vid_mid, ct_mid,
     normed1, inverse1, rot_b, proj,
-    qkv_snd, qkv_rcv, kx, qx, vx,
+    qkv_snd, qkv_rcv, beside_snd, fold, kx, qx, vx,
     att_snd, att_rcv, att1, top, aot, daz,
     hidp, normed2, proj2, att2_b, dproj_b,
     t_s, t_dp, t_p, t_ds,
-    ah_snd, ah_rcv, do_snd, do_rcv, qt, dkt, dvt, pq,
+    ah_snd, ah_rcv, do_snd, do_rcv, qt, dvt, pq,
     dk_snd, dk_rcv, dv_snd, dv_rcv, dq_snd, dq_rcv, dq_last, w_last, vg, dpt, adjt,
     r1_snd, r1_rcv, r1_z, r1_chunk, r1_out,
     r2_snd, r2_rcv, r2_z, r2_chunk, terms,
@@ -220,6 +220,14 @@
                 bd32[pl.ds(4 * m + s, NBLOCK, stride=BLOCK), :] = jnp.where(own, group(wide, s), 0.0)
         bd[index] = bd32[...].astype(BF16)
 
+    shape = (512, 384)
+    source, target = rows(shape), lanes(shape)
+    quarter, lane_in = source >> 7, source & 127
+    to_pair = jnp.where(lane_in < 64, (quarter & 1) * 128 + (quarter >> 1) * 64 + lane_in, -1)
+    to_last = jnp.where(jnp.logical_and(lane_in >= 64, lane_in < 88), 256 + quarter * 32 + lane_in - 64, -1)
+    hit = jnp.logical_or(target == to_pair, target == to_last)
+    fold[...] = jnp.where(hit, 1.0, 0.0).astype(BF16)
+
     early[0].wait()
     normed, _ = normalize(vid[...].reshape(TOKENS, D).astype(F32))
     early[1].wait()
@@ -249,13 +257,19 @@
         low = (jnp.where(lane < 72, q, k) * qscale).astype(BF16)
         high = jnp.where(lane < 16, k, jnp.where(lane < 88, v, 0.0)).astype(BF16)
         for f in range(2):
-            qkv_snd[f * HEADS + h, :, 0:128] = low[64 * f : 64 * (f + 1)]
-            qkv_snd[f * HEADS + h, :, 128:256] = high[64 * f : 64 * (f + 1)]
+            item = f * HEADS + h
+            qkv_snd[item, 0:64] = low[64 * f : 64 * (f + 1)]
+            for e in range(4):
+                at = 64 * f + 16 * e
+                beside_snd[16 * item : 16 * item + 16, 128 * e : 128 * e + 128] = high[at : at + 16]
+    folded = dot(beside_snd[...], fold[...]).astype(BF16)
+    for part in range(3):
+        qkv_snd[:, 64 + 16 * part : 80 + 16 * part] = group(folded, part).reshape(PWAYS, 16, 128)
 
     pl.semaphore_wait(barrier, len(near))
 
     for n, step in enumerate(SLOTS):
-        dst = qkv_rcv.at[pl.ds(64 * n, 64)]
+        dst = qkv_rcv.at[n]
         if any(step):
             zz, jj = ahead(step)
             remote(qkv_snd.at[jj], dst, 2, (zz, jj), qkv_sems.at[n // 8])
@@ -304,7 +318,19 @@
 
     def prepare(i, carry):
         at = pl.ds(pl.multiple_of(i * 256, 256), 256)
-        t0, t1 = qkv_rcv[at, 0:128].astype(F32), qkv_rcv[at, 128:256].astype(F32)
+        low, high = [], []
+        for m in range(4):
+            slot = qkv_rcv[4 * i + m].astype(F32)
+            low.append(slot[0:64])
+            mid, last = slot[64:96], slot[96:112]
+            high.append(
+                jnp.where(
+                    lanes((64, 128)) < 64,
+                    jnp.concatenate([mid, roll(mid, 64)], axis=0),
+                    jnp.concatenate([roll(last, 64 - 32 * e) for e in range(4)], axis=0),
+                )
+            )
+        t0, t1 = jnp.concatenate(low, axis=0), jnp.concatenate(high, axis=0)
         k = roll(jnp.where(lane2 >= 72, t0, t1), -72)
         kx[at, :] = jnp.where(lane2 < 72, k, ones).astype(BF16)
         vx[at, :] = jnp.where(lane2 < 72, roll(t1, -16), ones).astype(BF16)
@@ -312,17 +338,17 @@
         return carry
 
     for g in range(4):
-        wait_all(qkv_sems.at[g], qkv_rcv.at[pl.ds(512 * g, 512)])
+        wait_all(qkv_sems.at[g], qkv_rcv.at[pl.ds(8 * g, 8)])
         lax.fori_loop(2 * g, 2 * g + 2, prepare, 0)
 
-    def attend(i, carry):
-        spans = [pl.ds(pl.multiple_of(i * 512 + s * 256, 256), 256) for s in range(2)]
+    def attend_span(start, count):
+        spans = [pl.ds(start + s * 256, 256) for s in range(count)]
         highs = []
         for s, at in enumerate(spans):
             scores = dot_nt(qx[at, :], kx[...])
             highs.append(jnp.max(scores, axis=-1, keepdims=True))
             pq[256 * s : 256 * s + 256, :] = jnp.exp2(scores - highs[-1]).astype(BF16)
-        both_out = dot(pq[0:512, :], vx[...])
+        both_out = dot(pq[0 : 256 * count, :], vx[...])
         for s, (at, high_score) in enumerate(zip(spans, highs)):
             out = both_out[256 * s : 256 * s + 256]
             total = out[:, 72:73]
@@ -337,23 +363,31 @@
             )
             qx[at, :] = new.astype(BF16)
 
-        for ii in range(4):
+    def send_attended(slots):
+        for n in slots:
+            for d in (2, 1, 3, 0):
+                zz, jj = zs[d], behind(SLOTS[n])[1]
+                src = att_snd.at[pl.ds(pl.multiple_of(64 * n + 16 * zz, 16), 16)]
+                dst = att_rcv.at[2 * z + (j >> 4), j & 15]
+                if d or any(SLOTS[n]):
+                    remote(src, dst, 3, (zz, jj))
+                else:
+                    local(src, dst, recv_sems.at[3])
+
+    def attend(i, carry):
+        attend_span(pl.multiple_of(i * 512, 512), 2)
+        for ii in range(1, 4):
 
             @pl.when(i == ii)
             def _():
-                for n in range(8 * ii, 8 * ii + 8):
-                    for d in (2, 1, 3, 0):
-                        zz, jj = zs[d], behind(SLOTS[n])[1]
-                        src = att_snd.at[pl.ds(pl.multiple_of(64 * n + 16 * zz, 16), 16)]
-                        dst = att_rcv.at[2 * z + (j >> 4), j & 15]
-                        if d or any(SLOTS[n]):
-                            remote(src, dst, 3, (zz, jj))
-                        else:
-                            local(src, dst, recv_sems.at[3])
+                send_attended(range(8 * ii, 8 * ii + 8))
 
         return carry
 
-    lax.fori_loop(0, 4, attend, 0)
+    for half in range(2):
+        attend_span(256 * half, 1)
+        send_attended(range(4 * half, 4 * half + 4))
+    lax.fori_loop(1, 4, attend, 0)
 
     wait_all(recv_sems.at[0], vid_mid)
     wait_all(recv_sems.at[3], att_rcv)
@@ -583,11 +617,7 @@
             tile = dq[:, 128 * (m // 2) : 128 * (m // 2) + 128]
             dq_snd[8 * group_ + m] = beside(tile[0:32], tile[32:64], m % 2).astype(BF16)
         dq_last[:, group_ * 512 : group_ * 512 + 512] = dq[64:72]
-        dk = dot(qt[:, at], ds)
-        if group_ == 0:
-            dkt[...] = dk
-        else:
-            dkt[...] += dk
+        pq[at, :] = ds
         send_back(dq_snd, dq_rcv, 13, range(8 * group_, 8 * group_ + 8))
 
     def send_back(snd, rcv, phase, slots):
@@ -609,11 +639,19 @@
     for group_ in (1, 2, 3):
         attend_back(group_)
 
-    for n in range(PWAYS):
-        at = slice(128 * (n // 2), 128 * (n // 2) + 128)
-        rest = [dkt[48:72, at] * LN2, dq_last[:, at], dvt[64:72, at], jnp.zeros((8, 128), F32)]
-        dk_snd[n] = beside(dkt[0:48, at] * LN2, jnp.concatenate(rest, axis=0), n % 2).astype(BF16)
-    send_back(dk_snd, dk_rcv, 6, range(PWAYS))
+    def key_gradient(group_):
+        return dot(qt[...], pq[:, 512 * group_ : 512 * group_ + 512]) * LN2
+
+    dk = key_gradient(0)
+    for group_ in range(4):
+        following = key_gradient(group_ + 1) if group_ < 3 else None
+        for m in range(8):
+            n = 8 * group_ + m
+            at, here = slice(128 * (n // 2), 128 * (n // 2) + 128), slice(128 * (m // 2), 128 * (m // 2) + 128)
+            rest = [dk[48:72, here], dq_last[:, at], dvt[64:72, at], jnp.zeros((8, 128), F32)]
+            dk_snd[n] = beside(dk[0:48, here], jnp.concatenate(rest, axis=0), n % 2).astype(BF16)
+        send_back(dk_snd, dk_rcv, 6, range(8 * group_, 8 * group_ + 8))
+        dk = following
 
     reduce_second(r1_rcv, r1_z, owns1, 7)
 
@@ -788,7 +826,7 @@
         vm((4, BLOCK, BLOCK, NBLOCK), F32), vm((D, 128), F32), vm((4, D, 128), BF16),
         vm((2, 64, D), BF16), vm((2, 64, D), BF16), vm((FRAMES, 16, D), BF16), vm((FRAMES, 16, D), BF16),
         vm((D, TOKENS), F32), vm((8, TOKENS), F32), vm((TOKENS, D), BF16), vm((TOKENS, 3 * D), F32),
-        vm((PWAYS, 64, 256), BF16), vm((PATCHES, 256), BF16),
+        vm((PWAYS, 112, 128), BF16), vm((PWAYS, 112, 128), BF16), vm((512, 512), BF16), vm((512, 384), BF16),
         vm((PATCHES, 128), BF16), vm((PATCHES, 128), BF16), vm((PATCHES, 128), BF16),
         vm((PATCHES, 128), BF16), vm((FRAMES, HEADS, 16, 128), BF16), vm((TOKENS, D), BF16),
         vm((TOKENS, D), F32), vm((TOKENS, D), BF16), vm((TOKENS, D + 128), BF16),
@@ -798,7 +836,7 @@
         vm((HEADS, TOKENS, TOKENS), BF16), vm((HEADS, TOKENS, TOKENS), BF16),
         vm((FRAMES, 16, D), BF16), vm((2, 64, D), BF16),
         vm((FRAMES, HEADS, 16, 128), BF16), vm((PATCHES, 128), BF16),
-        vm((80, PATCHES), BF16), vm((80, PATCHES), F32), vm((80, PATCHES), F32), vm((PATCHES, PATCHES), BF16),
+        vm((80, PATCHES), BF16), vm((80, PATCHES), F32), vm((PATCHES, PATCHES), BF16),
         vm((PWAYS, 48, 128), BF16), vm((PWAYS, 48, 128), BF16), vm((PWAYS, 32, 128), BF16), vm((PWAYS, 32, 128), BF16),
         vm((PWAYS, 32, 128), BF16), vm((PWAYS, 32, 128), BF16), vm((8, PATCHES), F32), vm((2, D, 128), BF16),
         vm((2, 64, D), BF16),

time: 90.7 us -> 90 us (level)
  no operation moved by 1% of the time
where the time goes in v4:
time: 90 us; the launch traced here: 89.9 us
  Pallas kernels  89 us (99%)
    pallas_call x1, Pallas kernels, per_device(): pl.pallas_call(kernel, out_shape=(jax.ShapeDtypeStruct((2, 64, D), BF16),...  85.9 us
    pallas_call x1, Pallas kernels, per_device(): pl.pallas_call(unpack_kernel, out_shape=(jax.ShapeDtypeStruct((2, 64, D),...  3.09 us

profile of v4, /device:TPU:1, one launch (start us, length us, event | category | flops | bytes accessed | tf_op | source)
XLA Modules:
  0.0 89.9 jit_solution(11442124864557966533)
XLA Ops:
  0.6 85.9 %block_backward.1 = (bf16[2,64,1152]{2,1,0:T(8,128)(2,1)}, f32[3,32,32,36]{3,2,1,0:T(8,128)}, bf16[288,128]{1,0:T(8,128)(2,1)}) custom-call(s32[8]{0:T(128)} %mask_ref.1, bf16[2,64,1152]{2,1,0:T(8,128)(2,1)} %video.1, bf16[2,64,1152]{2,1,0:T(8,128)(2,1)} %cotangent.1, bf16[1152,3456]{1,0:T(8,128)(2,1)} %wsp_h.1, bf16[1152,1152]{1,0:T(8,128)(2,1)} %wso_h.1, ...), custom_call_target="tpu_custom_call" | custom-call | tf_op jit(solution)/shard_map/block_backward/pallas_call | solution.py:852
  86.6 3.1 %unpack_terms.1 = (bf16[2,64,1152]{2,1,0:T(8,128)(2,1)}, f32[32,32,36]{2,1,0:T(8,128)}, f32[32,32,36]{2,1,0:T(8,128)}, f32[32,32,36]{2,1,0:T(8,128)}, f32[32,32,36]{2,1,0:T(8,128)}) custom-call(bf16[288,128]{1,0:T(8,128)(2,1)} %get-tuple-element.13.sin_h, f32[3,32,32,36]{3,2,1,0:T(8,128)} %get-tuple-element.14.terms_h, ...), custom_call_target="tpu_custom_call" | custom-call | tf_op jit(solution)/shard_map/unpack_terms/pallas_call | solution.py:871

commit v5 on v4

--- a/solution.py
+++ b/solution.py
@@ -148,12 +148,12 @@
     normed1, inverse1, rot_b, proj,
     qkv_snd, qkv_rcv, beside_snd, fold, kx, qx, vx,
     att_snd, att_rcv, att1, top, aot, daz,
-    hidp, normed2, proj2, att2_b, dproj_b,
+    normed2, proj2, att2_b, dproj_b,
     t_s, t_dp, t_p, t_ds,
     ah_snd, ah_rcv, do_snd, do_rcv, qt, dvt, pq,
     dk_snd, dk_rcv, dv_snd, dv_rcv, dq_snd, dq_rcv, dq_last, w_last, vg, dpt, adjt,
     r1_snd, r1_rcv, r1_z, r1_chunk, r1_out,
-    r2_snd, r2_rcv, r2_z, r2_chunk, terms,
+    r2_snd, r2_rcv, r2_z, r2_chunk, r3_snd, r3_rcv, r3_z, r3_chunk, terms,
     load_sems, out_sems, send_sems, recv_sems, qkv_sems, do_sems,
 ):
     z = lax.axis_index("frame")
@@ -418,12 +418,9 @@
     rot_b[...] = rotate(normed.astype(BF16), bd.at[2]).astype(BF16)
     late[6].wait()
 
-    def project2(c, carry):
-        at = pl.ds(pl.multiple_of(c * D, 128), D)
+    for c in range(3):
+        at = slice(c * D, (c + 1) * D)
         proj2[:, at] = dot(rot_b[...], wtp[:, at]).astype(BF16)
-        return carry
-
-    lax.fori_loop(0, 3, project2, 0)
 
     square = (TOKENS, TOKENS)
     same_patch = rows(square) % 16 == lanes(square) % 16
@@ -479,10 +476,9 @@
     for section in range(3):
         gather(section, dproj_b, section * D)
 
-    for c in range(3):
-        at = slice(c * 384, (c + 1) * 384)
-        hidp[:, at] = dot_nt(dproj_b[...], wtp[at, :])
-    adj_rot2 = hidp[...].astype(BF16)
+    adj_rot2 = jnp.concatenate(
+        [dot_nt(dproj_b[...], wtp[c * 384 : (c + 1) * 384, :]).astype(BF16) for c in range(3)], axis=1
+    )
     adj_normed = rotate_transposed(adj_rot2, bd.at[2])
     adj_hidden = top[...] + normalize_backward(adj_normed, normed2[...], inverse2)
     adj_hidden_b = adj_hidden.astype(BF16)
@@ -705,22 +701,28 @@
         full = jnp.where(mask, dot_nt(normed1[at].astype(BF16), adjt[at].astype(BF16)), 0.0)
         packed.append(full[0:32] + full[32:64] + full[64:96] + full[96:128])
     flat = jnp.concatenate(packed, axis=0).astype(BF16)
-    for o in range(6):
-        r2_snd[o] = flat[48 * o : 48 * o + 48]
+    for o in range(8):
+        r2_snd[o] = flat[32 * o : 32 * o + 32]
+    for o in range(2):
+        r3_snd[o] = flat[256 + 16 * o : 272 + 16 * o]
     owner = 2 * px + pc
-    owns2 = owner < 6
+    more = (owner & 3) == 0
     row = [s for s in SLOTS if s[1] == 0]
     sheet = [s for s in SPACE if s[0] == 0 and s[2] == 0]
     for step in row:
         zz, jj = ahead(step)
         there = 2 * (jj >> 3) + (jj & 1)
-
-        @pl.when(there < 6)
+        if any(step):
+            remote(r2_snd.at[there], r2_rcv.at[owner], 10, (zz, jj))
+        else:
+            local(r2_snd.at[there], r2_rcv.at[owner], recv_sems.at[10])
+
+        @pl.when((there & 3) == 0)
         def _():
             if any(step):
-                remote(r2_snd.at[there], r2_rcv.at[owner], 10, (zz, jj))
+                remote(r3_snd.at[there >> 2], r3_rcv.at[owner], 14, (zz, jj))
             else:
-                local(r2_snd.at[there], r2_rcv.at[owner], recv_sems.at[10])
+                local(r3_snd.at[there >> 2], r3_rcv.at[owner], recv_sems.at[14])
 
     adj_normed = jnp.concatenate(
         [
@@ -737,13 +739,18 @@
     vg[...] = grad.astype(BF16).reshape(2, 64, D)
     vg_out = pltpu.make_async_copy(vg, vg_ref, out_sems.at[0])
     vg_out.start()
-    @pl.when(owns2)
+    def sheet_sum(rcv, zbuf, phase_in, phase):
+        wait_all(recv_sems.at[phase_in], rcv)
+        own = 4 * z + py
+        zbuf[own] = jnp.sum(rcv[...].astype(F32), axis=0).astype(BF16)
+        for step in sheet:
+            remote(zbuf.at[own], zbuf.at[own], phase, ahead(step))
+
+    sheet_sum(r2_rcv, r2_z, 10, 11)
+
+    @pl.when(more)
     def _():
-        wait_all(recv_sems.at[10], r2_rcv)
-        own = 4 * z + py
-        r2_z[own] = jnp.sum(r2_rcv[...].astype(F32), axis=0).astype(BF16)
-        for step in sheet:
-            remote(r2_z.at[own], r2_z.at[own], 11, ahead(step))
+        sheet_sum(r3_rcv, r3_z, 14, 16)
 
     wait_all(send_sems.at[0], vid_mid.at[pl.ds(0, 6)])
     wait_all(send_sems.at[1], ct_mid.at[pl.ds(0, 6)])
@@ -755,16 +762,20 @@
     wait_all(send_sems.at[15], dv_snd.at[pl.ds(0, PWAYS - 1)])
     wait_all(send_sems.at[13], dq_snd.at[pl.ds(0, PWAYS - 1)])
     wait_all(recv_sems.at[9], r1_out)
-    @pl.when(owns2)
-    def _():
-        wait_all(recv_sems.at[11], r2_z.at[pl.ds(0, 15)])
-        r2_chunk[...] = (jnp.sum(r2_z[...].astype(F32), axis=0) / 128.0).astype(BF16)
-        dst = red_ref.at[pl.ds(pl.multiple_of(48 * owner, 16), 48)]
+    def row_spread(zbuf, chunk, dst, phase_in, phase):
+        wait_all(recv_sems.at[phase_in], zbuf.at[pl.ds(0, 15)])
+        chunk[...] = (jnp.sum(zbuf[...].astype(F32), axis=0) / 128.0).astype(BF16)
         for step in row:
             if any(step):
-                remote(r2_chunk, dst, 12, ahead(step))
+                remote(chunk, dst, phase, ahead(step))
             else:
-                local(r2_chunk, dst, recv_sems.at[12])
+                local(chunk, dst, recv_sems.at[phase])
+
+    row_spread(r2_z, r2_chunk, red_ref.at[pl.ds(pl.multiple_of(32 * owner, 32), 32)], 11, 12)
+
+    @pl.when(more)
+    def _():
+        row_spread(r3_z, r3_chunk, red_ref.at[pl.ds(pl.multiple_of(256 + 16 * (owner >> 2), 16), 16)], 16, 17)
 
     tools = layout_tools()
     for n in range(3):
@@ -772,17 +783,22 @@
     red1 = pltpu.make_async_copy(terms, terms_ref, out_sems.at[1])
     red1.start()
     reduce_sent(r1_snd, r1_rcv, r1_z, 27, owns1, 7)
-    @pl.when(owns2)
+    wait_all(send_sems.at[10], r2_snd.at[pl.ds(0, 7)])
+    wait_all(send_sems.at[11], r2_z.at[pl.ds(0, 15)])
+    wait_all(send_sems.at[12], r2_rcv.at[pl.ds(0, 7)])
+
+    @pl.when(more)
     def _():
-        wait_all(send_sems.at[10], r2_snd.at[pl.ds(0, 5)])
-        wait_all(send_sems.at[11], r2_z.at[pl.ds(0, 15)])
-        wait_all(send_sems.at[12], r2_rcv.at[pl.ds(0, 7)])
-
-    @pl.when(jnp.logical_not(owns2))
+        wait_all(send_sems.at[14], r3_snd.at[0])
+        wait_all(send_sems.at[16], r3_z.at[pl.ds(0, 15)])
+        wait_all(send_sems.at[17], r3_rcv.at[pl.ds(0, 7)])
+
+    @pl.when(jnp.logical_not(more))
     def _():
-        wait_all(send_sems.at[10], r2_snd)
-
-    wait_all(recv_sems.at[12], red_ref)
+        wait_all(send_sems.at[14], r3_snd)
+
+    wait_all(recv_sems.at[12], red_ref.at[pl.ds(0, 256)])
+    wait_all(recv_sems.at[17], red_ref.at[pl.ds(256, 32)])
     red1.wait()
     vg_out.wait()
 
@@ -830,7 +846,7 @@
         vm((PATCHES, 128), BF16), vm((PATCHES, 128), BF16), vm((PATCHES, 128), BF16),
         vm((PATCHES, 128), BF16), vm((FRAMES, HEADS, 16, 128), BF16), vm((TOKENS, D), BF16),
         vm((TOKENS, D), F32), vm((TOKENS, D), BF16), vm((TOKENS, D + 128), BF16),
-        vm((TOKENS, D), F32), vm((TOKENS, D), F32), vm((TOKENS, 3 * D), BF16),
+        vm((TOKENS, D), F32), vm((TOKENS, 3 * D), BF16),
         vm((TOKENS, D), BF16), vm((TOKENS, 3 * D), BF16),
         vm((HEADS, TOKENS, TOKENS), F32), vm((HEADS, TOKENS, TOKENS), F32),
         vm((HEADS, TOKENS, TOKENS), BF16), vm((HEADS, TOKENS, TOKENS), BF16),
@@ -843,9 +859,10 @@
         vm((3 * D, TOKENS), BF16), vm((D, TOKENS), F32),
         vm((27, 32, 128), BF16), vm((PWAYS, 32, 128), BF16), vm((ZWAYS, 32, 128), F32),
         vm((32, 128), BF16), vm((3 * ROWS, 128), BF16),
-        vm((6, 48, 128), BF16), vm((8, 48, 128), BF16), vm((16, 48, 128), BF16),
-        vm((48, 128), BF16), vm((3, BLOCK, BLOCK, NBLOCK), F32),
-        dma((12,)), dma((3,)), dma((16,)), dma((16,)), dma((4,)), dma((4,)),
+        vm((8, 32, 128), BF16), vm((8, 32, 128), BF16), vm((16, 32, 128), BF16), vm((32, 128), BF16),
+        vm((2, 16, 128), BF16), vm((8, 16, 128), BF16), vm((16, 16, 128), BF16), vm((16, 128), BF16),
+        vm((3, BLOCK, BLOCK, NBLOCK), F32),
+        dma((12,)), dma((3,)), dma((18,)), dma((18,)), dma((4,)), dma((4,)),
     ]
     anyspec = pl.BlockSpec(memory_space=pl.ANY)
     blocks = [r.transpose(1, 2, 0) for r in (spatial_inward, spatial_outward, temporal_inward, temporal_outward)]

time: 90 us -> 89.4 us (level)
  no operation moved by 1% of the time
where the time goes in v5:
time: 89.4 us; the launch traced here: 89.3 us
  Pallas kernels  88.4 us (99%)
    pallas_call x1, Pallas kernels, per_device(): pl.pallas_call(kernel, out_shape=(jax.ShapeDtypeStruct((2, 64, D), BF16),...  85.3 us
    pallas_call x1, Pallas kernels, per_device(): pl.pallas_call(unpack_kernel, out_shape=(jax.ShapeDtypeStruct((2, 64, D),...  3.09 us

profile of v5, /device:TPU:1, one launch (start us, length us, event | category | flops | bytes accessed | tf_op | source)
XLA Modules:
  0.0 89.3 jit_solution(8733810421464010736)
XLA Ops:
  0.6 85.3 %block_backward.1 = (bf16[2,64,1152]{2,1,0:T(8,128)(2,1)}, f32[3,32,32,36]{3,2,1,0:T(8,128)}, bf16[288,128]{1,0:T(8,128)(2,1)}) custom-call(s32[8]{0:T(128)} %mask_ref.1, bf16[2,64,1152]{2,1,0:T(8,128)(2,1)} %video.1, bf16[2,64,1152]{2,1,0:T(8,128)(2,1)} %cotangent.1, bf16[1152,3456]{1,0:T(8,128)(2,1)} %wsp_h.1, bf16[1152,1152]{1,0:T(8,128)(2,1)} %wso_h.1, ...), custom_call_target="tpu_custom_call" | custom-call | tf_op jit(solution)/shard_map/block_backward/pallas_call | solution.py:869
  86.0 3.1 %unpack_terms.1 = (bf16[2,64,1152]{2,1,0:T(8,128)(2,1)}, f32[32,32,36]{2,1,0:T(8,128)}, f32[32,32,36]{2,1,0:T(8,128)}, f32[32,32,36]{2,1,0:T(8,128)}, f32[32,32,36]{2,1,0:T(8,128)}) custom-call(bf16[288,128]{1,0:T(8,128)(2,1)} %get-tuple-element.13.sin_h, f32[3,32,32,36]{3,2,1,0:T(8,128)} %get-tuple-element.14.terms_h, ...), custom_call_target="tpu_custom_call" | custom-call | tf_op jit(solution)/shard_map/unpack_terms/pallas_call | solution.py:888

commit v6 on v5

--- a/solution.py
+++ b/solution.py
@@ -493,7 +493,7 @@
         piece = jnp.where(lane < 72, roll(first, -off), 0.0).astype(BF16)
         do_snd[:, h] = piece.reshape(FRAMES, 16, 128)
 
-    for step in [slot[:3] + (d,) for slot in SLOTS for d in (2, 1, 3, 0)]:
+    for step in [SLOTS[8 * g + m][:3] + (d,) for g in (3, 2, 1, 0) for m in range(8) for d in (2, 1, 3, 0)]:
         zz, jj = ahead(step)
         src = do_snd.at[2 * zz + (jj >> 4), jj & 15]
         n = SLOT_OF[step[:3]]
@@ -594,7 +594,7 @@
     def value_gradient(group_):
         at = pl.ds(group_ * 512, 512)
         dv = dot(do_rcv[at, :].astype(F32).T[0:80].astype(BF16), pq[at, :])
-        if group_ == 0:
+        if group_ == 3:
             dvt[...] = dv
         else:
             dvt[...] += dv
@@ -623,16 +623,16 @@
             else:
                 local(snd.at[n], rcv.at[j], recv_sems.at[phase])
 
-    for group_ in range(4):
+    for group_ in (3, 2, 1, 0):
         wait_all(do_sems.at[group_], do_rcv.at[pl.ds(512 * group_, 512)])
         value_gradient(group_)
-        if group_ == 0:
-            attend_back(0)
+        if group_ >= 2:
+            attend_back(group_)
     for n in range(PWAYS):
         at = slice(128 * (n // 2), 128 * (n // 2) + 128)
         dv_snd[n] = beside(dvt[0:32, at], dvt[32:64, at], n % 2).astype(BF16)
     send_back(dv_snd, dv_rcv, 15, range(PWAYS))
-    for group_ in (1, 2, 3):
+    for group_ in (1, 0):
         attend_back(group_)
 
     def key_gradient(group_):

time: 89.4 us -> 87.9 us (0.983)
  Pallas kernels: 88.4 us -> 86.9 us
    pallas_call x1, Pallas kernels: 85.3 us -> 83.8 us  [per_device(): pl.pallas_call(kernel, out_shape=(jax.ShapeDtypeStruct((2, 64, D), BF16),...]
where the time goes in v6:
time: 87.9 us; the launch traced here: 87.7 us
  Pallas kernels  86.9 us (99%)
    pallas_call x1, Pallas kernels, per_device(): pl.pallas_call(kernel, out_shape=(jax.ShapeDtypeStruct((2, 64, D), BF16),...  83.8 us
    pallas_call x1, Pallas kernels, per_device(): pl.pallas_call(unpack_kernel, out_shape=(jax.ShapeDtypeStruct((2, 64, D),...  3.09 us

profile of v6, /device:TPU:1, one launch (start us, length us, event | category | flops | bytes accessed | tf_op | source)
XLA Modules:
  0.0 87.7 jit_solution(6590124917756902379)
XLA Ops:
  0.6 83.8 %block_backward.1 = (bf16[2,64,1152]{2,1,0:T(8,128)(2,1)}, f32[3,32,32,36]{3,2,1,0:T(8,128)}, bf16[288,128]{1,0:T(8,128)(2,1)}) custom-call(s32[8]{0:T(128)} %mask_ref.1, bf16[2,64,1152]{2,1,0:T(8,128)(2,1)} %video.1, bf16[2,64,1152]{2,1,0:T(8,128)(2,1)} %cotangent.1, bf16[1152,3456]{1,0:T(8,128)(2,1)} %wsp_h.1, bf16[1152,1152]{1,0:T(8,128)(2,1)} %wso_h.1, ...), custom_call_target="tpu_custom_call" | custom-call | tf_op jit(solution)/shard_map/block_backward/pallas_call | solution.py:869
  84.5 3.1 %unpack_terms.1 = (bf16[2,64,1152]{2,1,0:T(8,128)(2,1)}, f32[32,32,36]{2,1,0:T(8,128)}, f32[32,32,36]{2,1,0:T(8,128)}, f32[32,32,36]{2,1,0:T(8,128)}, f32[32,32,36]{2,1,0:T(8,128)}) custom-call(bf16[288,128]{1,0:T(8,128)(2,1)} %get-tuple-element.13.sin_h, f32[3,32,32,36]{3,2,1,0:T(8,128)} %get-tuple-element.14.terms_h, ...), custom_call_target="tpu_custom_call" | custom-call | tf_op jit(solution)/shard_map/unpack_terms/pallas_call | solution.py:888
